TPU v7x, 512 devices: a whole 4x4x16 slice. The times are simulated.
512 devices in a mesh: fsdp: 32 (over y, x, core), tp: 16 (over z).
Axes of the slice: x: 4, y: 4, z: 16, core: 2. Of those that a mesh axis runs over, the one named last changes fastest.
Arguments:
- gradient: float32 [18432, 7168], P('fsdp', 'tp'), may hold values from -600 to 600
- momentum: float32 [18432, 7168], P('fsdp', 'tp'), may hold values from -6 to 6
- start_basis: float32 [7168, 256], P('tp'), may hold values from -6 to 6
Outputs:
- update: float32 [18432, 7168], P('fsdp', 'tp')
- new_momentum: float32 [18432, 7168], P('fsdp', 'tp')
- directions: float32 [7168, 256], P('tp')
All inputs are finite; a program needn't handle non-finite values.
Results may differ from a plain program's by a relative error of at most 0.00011.
Values sent between devices are 32-bit elements; how exact they have to be, the bound alone decides.
No kernel may reach another device: no remote copies, remote signals or barrier semaphores. Data moves between devices by JAX's collectives and lax.ppermute only.
A program may use at most 64 MiB of HBM per device.

v0:
```python
import math

import jax
import jax.numpy as jnp
from jax import lax
from jax.sharding import PartitionSpec as P

M_ROWS = 18432
N_COLS = 7168
RANK = 256
ITERS = 2


decay_rate = 0.95
epsilon = 1e-06


def local(gradient, momentum, start_basis):
    highest = lax.Precision.HIGHEST
    combined = momentum + gradient
    current = start_basis
    for iteration in range(ITERS):
        partial_proj = jnp.dot(combined, current, precision=highest)
        projected = lax.psum(partial_proj, "tp")
        gram_matrix = lax.psum(jnp.dot(projected.T, projected, precision=highest), "fsdp")
        factor = jnp.linalg.cholesky(gram_matrix)
        orthonormal = lax.linalg.triangular_solve(
            factor, projected, left_side=False, lower=True, transpose_a=True
        )
        reflected = lax.psum(jnp.dot(combined.T, orthonormal, precision=highest), "fsdp")
        current = reflected
    squares = lax.psum(jnp.sum(reflected * reflected, axis=0), "tp")
    mean_square = squares / N_COLS
    directions = reflected * lax.rsqrt(mean_square + epsilon)
    new_momentum = combined - (1.0 - decay_rate) * jnp.dot(
        orthonormal, reflected.T, precision=highest
    )
    update = math.sqrt(M_ROWS / RANK) * jnp.dot(orthonormal, directions.T, precision=highest)
    return (update, new_momentum, directions)


def solution(mesh):
    return jax.shard_map(
        local,
        mesh=mesh,
        in_specs=(P("fsdp", "tp"), P("fsdp", "tp"), P("tp", None)),
        out_specs=(P("fsdp", "tp"), P("fsdp", "tp"), P("tp", None)),
        check_vma=False,
    )
```

profile of v0, /device:TPU:1, one launch (start us, length us, event | category | flops | bytes accessed | tf_op | source)
XLA Modules:
  0.0 997.0 jit_solution(13249986341588441053)
XLA Ops:
  7.2 1.8 add.40
  9.0 3.0 fusion.32
  12.1 133.2 %all-reduce.8.cloned.1.call-done = f32[576,256]{1,0:T(8,128)} async-done(((f32[576,256]{1,0:T(8,128)}), f32[576,256]{1,0:T(8,128)}) %all-reduce.8.cloned.1.call-update) | async-done | bytes 589840 | tf_op jit(solution)/shard_map/psum | solution.py:24
  145.3 3.2 fusion.33
  148.5 0.6 all-reduce.12.cloned.1.call-start
  149.1 138.2 %all-reduce.10.cloned.1.call-done = f32[256,256]{0,1:T(8,128)} async-done(((f32[256,256]{0,1:T(8,128)}), f32[256,256]{0,1:T(8,128)}) %all-reduce.10.cloned.1.call-update) | async-done | bytes 262160 | tf_op jit(solution)/shard_map/psum | solution.py:25
  287.3 1.1 copy.7
  288.4 1.0 fusion.11
  289.4 11.7 %cholesky.130 = f32[128,128]{1,0:T(8,128)S(1)} custom-call(f32[128,128]{1,0:T(8,128)S(1)} %cholesky.194), custom_call_target="Cholesky" | custom-call | tf_op jit(solution)/shard_map/jit(cholesky)/cholesky | solution.py:26
  301.2 9.8 custom-call.13
  311.5 11.7 %cholesky.147 = f32[128,128]{1,0:T(8,128)S(1)} custom-call(f32[128,128]{1,0:T(8,128)S(1)} %convolution_subtract_fusion.3), custom_call_target="Cholesky" | custom-call | tf_op jit(solution)/shard_map/jit(cholesky)/cholesky | solution.py:26
  323.2 0.6 compare_reduce_fusion.2
  325.2 4.0 while.4
  325.4 0.6 fusion.58
  326.0 1.3 bitcast_dynamic-update-slice_fusion.4
  327.3 0.6 fusion.58
  327.9 1.3 bitcast_dynamic-update-slice_fusion.4
  329.2 19.7 %custom-call.14 = f32[2,128,128]{1,2,0:T(8,128)S(1)} custom-call(f32[2,128,128]{2,1,0:T(8,128)S(1)} %get-tuple-element.19), custom_call_target="InvertDiagBlocksLowerTriangular" | custom-call | tf_op jit(solution)/shard_map/triangular_solve/custom-call.0 | solution.py:27
  349.3 0.4 convolution_subtract_fusion.1
  349.7 0.4 fusion.16
  350.1 2.0 fusion.1
  352.2 133.4 %all-reduce.12.cloned.1.call-done = f32[448,256]{1,0:T(8,128)} async-done(((f32[448,256]{1,0:T(8,128)}), f32[448,256]{1,0:T(8,128)}) %all-reduce.12.cloned.1.call-update) | async-done | bytes 458768 | tf_op jit(solution)/shard_map/psum | solution.py:30
  485.6 4.0 fusion.34
  489.7 128.0 %all-reduce.14.cloned.1.call-done = f32[576,256]{1,0:T(8,128)} async-done(((f32[576,256]{1,0:T(8,128)}), f32[576,256]{1,0:T(8,128)}) %all-reduce.14.cloned.1.call-update) | async-done | bytes 589840 | tf_op jit(solution)/shard_map/psum | solution.py:24
  617.7 3.2 fusion.35
  621.1 138.0 %all-reduce.16.cloned.1.call-done = f32[256,256]{0,1:T(8,128)} async-done(((f32[256,256]{0,1:T(8,128)}), f32[256,256]{0,1:T(8,128)}) %all-reduce.16.cloned.1.call-update) | async-done | bytes 262160 | tf_op jit(solution)/shard_map/psum | solution.py:25
  759.1 1.1 copy.9
  760.2 1.0 fusion.10
  761.2 11.7 %cholesky.164 = f32[128,128]{1,0:T(8,128)S(1)} custom-call(f32[128,128]{1,0:T(8,128)S(1)} %cholesky.197), custom_call_target="Cholesky" | custom-call | tf_op jit(solution)/shard_map/jit(cholesky)/cholesky | solution.py:26
  773.0 0.6 compare_reduce_fusion.1
  773.6 9.8 custom-call.15
  783.9 11.7 %cholesky.181 = f32[128,128]{1,0:T(8,128)S(1)} custom-call(f32[128,128]{1,0:T(8,128)S(1)} %convolution_subtract_fusion.2), custom_call_target="Cholesky" | custom-call | tf_op jit(solution)/shard_map/jit(cholesky)/cholesky | solution.py:26
  795.7 0.6 compare_reduce_fusion
  797.7 4.3 while.5
  798.0 0.6 fusion.59
  798.5 1.4 bitcast_dynamic-update-slice_fusion.5
  800.0 0.6 fusion.59
  800.5 1.4 bitcast_dynamic-update-slice_fusion.5
  801.9 19.7 %custom-call.16 = f32[2,128,128]{1,2,0:T(8,128)S(1)} custom-call(f32[2,128,128]{2,1,0:T(8,128)S(1)} %get-tuple-element.20), custom_call_target="InvertDiagBlocksLowerTriangular" | custom-call | tf_op jit(solution)/shard_map/triangular_solve/custom-call.0 | solution.py:27
  822.0 0.4 convolution_subtract_fusion
  822.4 0.4 fusion.12
  822.8 2.0 fusion.5
  824.9 133.5 %all-reduce.18.cloned.1.call-done = f32[448,256]{1,0:T(8,128)} async-done(((f32[448,256]{1,0:T(8,128)}), f32[448,256]{1,0:T(8,128)}) %all-reduce.18.cloned.1.call-update) | async-done | bytes 458768 | tf_op jit(solution)/shard_map/psum | solution.py:30
  958.3 1.1 multiply_reduce_fusion
  959.4 24.8 %psum.55 = f32[256]{0:T(256)S(1)} all-reduce(f32[256]{0:T(256)S(1)} %multiply_reduce_fusion), channel_id=1, replica_groups=mesh['fsdp'=32,'tp'=16] {'tp'}, use_global_device_ids=true, to_apply=%region_11.14 | all-reduce | flops 256 | bytes 2048 | tf_op jit(solution)/shard_map/psum | solution.py:32
  984.3 1.1 broadcast_multiply_fusion
  985.3 2.3 convolution_multiply_fusion.1
  987.6 2.3 fusion
  (46 shorter events, 2.6 us)
Async XLA Ops:
  7.2 1.8 copy-start
  7.2 138.2 %all-reduce.8.cloned.1.call-start = ((), (), s32[]{:S(2)}) async-start(), calls=%async_computation | async-start | bytes 1179648 | tf_op jit(solution)/shard_map/psum | solution.py:24
  12.0 275.3 %all-reduce.10.cloned.1.call-start = ((), (), s32[]{:S(2)}) async-start(), calls=%async_computation.1 | async-start | bytes 524288 | tf_op jit(solution)/shard_map/psum | solution.py:25
  148.5 337.1 %all-reduce.12.cloned.1.call-start = ((), (), s32[]{:S(2)}) async-start(), calls=%async_computation.2 | async-start | bytes 917504 | tf_op jit(solution)/shard_map/psum | solution.py:30
  311.0 37.9 %copy-start.1 = (f32[576,256]{1,0:T(8,128)S(1)}, f32[576,256]{1,0:T(8,128)}, u32[]{:S(2)}) copy-start(f32[576,256]{1,0:T(8,128)} %all-reduce.8.cloned.1.call-done) | copy-start | bytes 1769476
  352.1 265.5 %all-reduce.14.cloned.1.call-start = ((), (), s32[]{:S(2)}) async-start(), calls=%async_computation.3 | async-start | bytes 1179648 | tf_op jit(solution)/shard_map/psum | solution.py:24
  489.7 269.4 %all-reduce.16.cloned.1.call-start = ((), (), s32[]{:S(2)}) async-start(), calls=%async_computation.4 | async-start | bytes 524288 | tf_op jit(solution)/shard_map/psum | solution.py:25
  620.9 337.5 %all-reduce.18.cloned.1.call-start = ((), (), s32[]{:S(2)}) async-start(), calls=%async_computation.5 | async-start | bytes 917504 | tf_op jit(solution)/shard_map/psum | solution.py:30
  783.4 38.2 %copy-start.2 = (f32[576,256]{1,0:T(8,128)S(1)}, f32[576,256]{1,0:T(8,128)}, u32[]{:S(2)}) copy-start(f32[576,256]{1,0:T(8,128)} %all-reduce.14.cloned.1.call-done) | copy-start | bytes 1769476
  985.3 4.6 copy-start.4
  985.3 2.3 copy-start.3
Sparse Core Ops, SparseCore 0:
  12.2 133.1 all-reduce.7
  149.5 137.8 all-reduce.9
  352.3 133.3 all-reduce.11
  489.8 127.8 all-reduce.13
  621.3 137.7 all-reduce.15
  825.0 133.3 all-reduce.17
where the time goes:
time: 1010 us; the launch traced here: 997 us
  waiting for transfers between devices  804 us (80%)
  other arithmetic  114 us (11%)
  matrix products  25.2 us (2%)
  blocking collectives  24.8 us (2%)
  between operations  17.2 us (2%)
    psum x2, waiting for transfers between devices, local(): lax.psum(jnp.dot(projected.T, projected, precision=highest), 'fsdp')  276 us
    psum x2, waiting for transfers between devices, local(): lax.psum(jnp.dot(combined.T, orthonormal, precision=highest), 'fsdp')  267 us
    psum x2, waiting for transfers between devices, local(): projected = lax.psum(partial_proj, 'tp')  261 us
    another operation x13, other arithmetic, local(): factor = jnp.linalg.cholesky(gram_matrix)  68.5 us
    another operation x5, other arithmetic, local(): lax.linalg.triangular_solve(factor, projected, left_side=False, lower=Tru...  39.4 us
    psum x1, blocking collectives, local(): squares = lax.psum(jnp.sum(reflected * reflected, axis=0), 'tp')  24.8 us
  transfers between devices with their start and end apart: 6, of which 6 were waited for; matrix products, arithmetic and copies ran while one was open for 0% of the time, Pallas kernels for 0%

commit v1 on v0

v1 whole, which is shorter than its diff:
```python
import math

import jax
import jax.numpy as jnp
from jax import lax
from jax.experimental import pallas as pl
from jax.experimental.pallas import tpu as pltpu
from jax.sharding import PartitionSpec as P

M_ROWS = 18432
N_COLS = 7168
RANK = 256
HALF = RANK // 2
FSDP = 32
TP = 16
ROWS = M_ROWS // FSDP
COLS = N_COLS // TP
BAND = 2 * ROWS // TP
SHARE = 40

decay_rate = 0.95
epsilon = 1e-06

F32 = jnp.float32
BF16 = jnp.bfloat16
HIGHEST = lax.Precision.HIGHEST
PANEL = 4

NN = (((1,), (0,)), ((), ()))
NT = (((1,), (1,)), ((), ()))
TN = (((0,), (0,)), ((), ()))


def split(x):
    high = x.astype(BF16)
    return high, (x - high.astype(F32)).astype(BF16)


def dot3(a, b, dims):
    one = lambda u, v: lax.dot_general(u, v, dims, preferred_element_type=F32)
    return one(a[0], b[0]) + (one(a[0], b[1]) + one(a[1], b[0]))


def dot6(a, b, dims):
    return lax.dot_general(a, b, dims, precision=HIGHEST, preferred_element_type=F32)


def call(kernel, out_shape, *args, flops=0, **kw):
    n_bytes = sum(x.size * x.dtype.itemsize for x in args)
    return pl.pallas_call(
        kernel,
        out_shape=out_shape,
        compiler_params=pltpu.CompilerParams(vmem_limit_bytes=48 * 2**20),
        cost_estimate=pl.CostEstimate(flops=flops, bytes_accessed=n_bytes, transcendentals=0),
        **kw,
    )(*args)


def shape(*dims, dtype=F32):
    return jax.ShapeDtypeStruct(dims, dtype)


def put_bands(ref, value):
    for i in range(value.shape[0] // BAND):
        for h in range(2):
            ref[2 * i + h] = value[i * BAND : (i + 1) * BAND, h * HALF : (h + 1) * HALF]


def get_bands(ref):
    halves = [ref[pl.ds(h, TP // 2, 2)] for h in range(2)]
    return jnp.concatenate([x.reshape(ROWS, HALF) for x in halves], axis=1)


def first_kernel(g_ref, m_ref, b_ref, high_ref, low_ref, out_ref):
    high, low = split(m_ref[...] + g_ref[...])
    high_ref[...] = high
    low_ref[...] = low
    put_bands(out_ref, dot3((high, low), split(b_ref[...]), NN))


def first(g, m, b):
    n = 4
    rows = ROWS // n
    block = pl.BlockSpec((rows, COLS), lambda i: (i, 0))
    return call(
        first_kernel,
        (shape(ROWS, COLS, dtype=BF16), shape(ROWS, COLS, dtype=BF16), shape(TP, BAND, HALF)),
        g,
        m,
        b,
        flops=6 * ROWS * COLS * RANK,
        grid=(n,),
        in_specs=[block, block, pl.BlockSpec((COLS, RANK), lambda i: (0, 0))],
        out_specs=[block, block, pl.BlockSpec((TP // n, BAND, HALF), lambda i: (i, 0, 0))],
    )


def fold_kernel(x_ref, out_ref):
    out_ref[...] = jnp.broadcast_to(jnp.sum(x_ref[...], axis=0, keepdims=True), out_ref.shape)


def all_sum(x, axis):
    terms = lax.all_to_all(x, axis, 0, 0)
    return lax.all_to_all(call(fold_kernel, shape(*x.shape), terms), axis, 0, 0)


def put_reflected(ref, c, p):
    for h in range(2):
        ref[h * COLS : (h + 1) * COLS, :] = c[:, h * HALF : (h + 1) * HALF]
    left, right = p[:, :HALF], p[:, HALF:]
    for i, (a, b) in enumerate(((left, left), (right, left), (right, right))):
        ref[2 * COLS + i * HALF : 2 * COLS + (i + 1) * HALF, :] = dot6(a, b, TN)


def get_reflected(ref):
    return jnp.concatenate([ref[h * COLS : (h + 1) * COLS, :] for h in range(2)], axis=1)


def reflect_kernel(high_ref, low_ref, p_ref, out_ref):
    p = get_bands(p_ref)
    put_reflected(out_ref, dot3((high_ref[...], low_ref[...]), split(p), TN), p)


def reflect(high, low, p):
    return call(reflect_kernel, shape(FSDP * SHARE, HALF), high, low, p, flops=6 * ROWS * COLS * RANK)


def project_kernel(high_ref, low_ref, c_ref, out_ref):
    put_bands(out_ref, dot3((high_ref[...], low_ref[...]), split(get_reflected(c_ref)), NN))


def project(high, low, c):
    return call(project_kernel, shape(TP, BAND, HALF), high, low, c, flops=6 * ROWS * COLS * RANK)


def second_reflect_kernel(high_ref, low_ref, p_ref, x_ref, p_out_ref, out_ref):
    p = dot6(get_bands(p_ref), x_ref[...], NT)
    p_out_ref[...] = p
    put_reflected(out_ref, dot3((high_ref[...], low_ref[...]), split(p), TN), p)


def second_reflect(high, low, p, x):
    return call(
        second_reflect_kernel,
        (shape(ROWS, RANK), shape(FSDP * SHARE, HALF)),
        high,
        low,
        p,
        x,
        flops=6 * ROWS * COLS * RANK,
    )


def inverse_factor_128(s):
    lanes = lambda v, k: jnp.broadcast_to(v[:, k : k + 1], (8, HALF))
    sublanes = lambda v, k: jnp.broadcast_to(v[k : k + 1, :], (8, HALF))
    n = HALF // 8
    a = [s[8 * v : 8 * v + 8, :] for v in range(n)]
    row_at = lax.broadcasted_iota(jnp.int32, (8, HALF), 0)
    col_at = lax.broadcasted_iota(jnp.int32, (8, HALF), 1)
    e = [jnp.where(col_at == row_at + 8 * v, 1.0, 0.0).astype(F32) for v in range(n)]
    out = []
    for k0 in range(0, HALF, PANEL):
        v0, s0 = k0 // 8, k0 % 8
        last = k0 + PANEL >= 8 * (v0 + 1)
        cols = {v: [lanes(a[v], k0 + j) for j in range(PANEL)] for v in range(v0, n)}
        rows = [sublanes(a[v0], s0 + j) for j in range(PANEL)]
        units = [sublanes(e[v0], s0 + j) for j in range(PANEL)]
        d = [[sublanes(cols[v0][j], s0 + i) for j in range(i + 1)] for i in range(PANEL)]
        factor = [[None] * PANEL for _ in range(PANEL)]
        inverse = [None] * PANEL
        for j in range(PANEL):
            t = d[j][j]
            for k in range(j):
                t = t - factor[j][k] * factor[j][k]
            r = lax.rsqrt(t)
            inverse[j] = r * (1.5 - 0.5 * t * (r * r))
            for i in range(j + 1, PANEL):
                t = d[i][j]
                for k in range(j):
                    t = t - factor[i][k] * factor[j][k]
                factor[i][j] = t * inverse[j]

        def solve(x):
            y = []
            for j in range(PANEL):
                t = x[j]
                for k in range(j):
                    t = t - factor[j][k] * y[k]
                y.append(t * inverse[j])
            return y

        rows, units = solve(rows), solve(units)
        out += [u[:1] for u in units]
        for v in range(v0 + 1 if last else v0, n):
            c = solve(cols[v])
            for j in range(PANEL):
                a[v] = a[v] - c[j] * rows[j]
                e[v] = e[v] - c[j] * units[j]
    return out


def store_rows(ref, at, rows):
    for i, row in enumerate(rows):
        ref[at + i : at + i + 1, :HALF] = row


def factor_kernel(g_ref, x_ref, t_ref):
    at = 2 * COLS
    g11, g21, g22 = (g_ref[at + i * HALF : at + (i + 1) * HALF, :] for i in range(3))
    store_rows(x_ref, 0, inverse_factor_128(g11))
    x_ref[:HALF, HALF:] = jnp.zeros((HALF, HALF), F32)
    x11 = x_ref[:HALF, :HALF]
    l21 = dot6(g21, x11, NT)
    store_rows(t_ref, 0, inverse_factor_128(g22 - dot6(l21, l21, NT)))
    x22 = t_ref[...]
    x_ref[HALF:, HALF:] = x22
    x_ref[HALF:, :HALF] = -dot6(x22, dot6(l21, x11, NN), NN)


def inverse_factor(reflected):
    return call(
        factor_kernel,
        shape(RANK, RANK),
        reflected,
        flops=2 * 10**10,
        scratch_shapes=[pltpu.VMEM((HALF, HALF), F32)],
    )


def basis_kernel(p_ref, c_ref, x_ref, q_ref, r_ref, s_ref):
    x = split(x_ref[...])
    q_ref[...] = dot3(split(p_ref[...]), x, NT)
    r = dot3(split(get_reflected(c_ref)), x, NT)
    r_ref[...] = r
    squares = jnp.sum(r * r, axis=0, keepdims=True)
    for h in range(2):
        half = squares[:, h * HALF : (h + 1) * HALF]
        s_ref[:, 4 * h : 4 * h + 4, :] = jnp.broadcast_to(half[None], (TP, 4, HALF))


def basis(p, c, x):
    return call(
        basis_kernel,
        (shape(ROWS, RANK), shape(COLS, RANK), shape(TP, 8, HALF)),
        p,
        c,
        x,
        flops=6 * (ROWS + COLS) * RANK * RANK,
    )


def momentum_kernel(g_ref, m_ref, q_ref, r_ref, out_ref):
    product = dot3(split(q_ref[...]), split(r_ref[...]), NT)
    out_ref[...] = (m_ref[...] + g_ref[...]) - (1.0 - decay_rate) * product


def update_kernel(q_ref, r_ref, s_ref, out_ref, d_ref):
    squares = jnp.sum(s_ref[...], axis=0)
    scale = lax.rsqrt(squares / N_COLS + epsilon)
    scale = jnp.concatenate([scale[:1], scale[4:5]], axis=1)
    d = r_ref[...] * scale
    d_ref[...] = d
    out_ref[...] = math.sqrt(M_ROWS / RANK) * dot3(split(q_ref[...]), split(d), NT)


def local(gradient, momentum, start_basis):
    high, low, p = first(gradient, momentum, start_basis)
    p = all_sum(p, "tp")
    c = reflect(high, low, p)
    c = all_sum(c.reshape(FSDP, SHARE, HALF), "fsdp").reshape(FSDP * SHARE, HALF)
    p = project(high, low, c)
    x = inverse_factor(c)
    p = all_sum(p, "tp")
    p, c = second_reflect(high, low, p, x)
    c = all_sum(c.reshape(FSDP, SHARE, HALF), "fsdp").reshape(FSDP * SHARE, HALF)
    x = inverse_factor(c)
    q, r, squares = basis(p, c, x)
    squares = lax.all_to_all(squares, "tp", 0, 0)
    flops = 6 * ROWS * COLS * RANK
    new_momentum = call(momentum_kernel, shape(ROWS, COLS), gradient, momentum, q, r, flops=flops)
    update, directions = call(
        update_kernel, (shape(ROWS, COLS), shape(COLS, RANK)), q, r, squares, flops=flops
    )
    return (update, new_momentum, directions)


def solution(mesh):
    return jax.shard_map(
        local,
        mesh=mesh,
        in_specs=(P("fsdp", "tp"), P("fsdp", "tp"), P("tp", None)),
        out_specs=(P("fsdp", "tp"), P("fsdp", "tp"), P("tp", None)),
        check_vma=False,
    )
```

time: 1010 us -> 285 us (0.28); the launches traced: 997 us -> 284 us
  waiting for transfers between devices: 804 us -> 16.3 us
  blocking collectives: 24.8 us -> 201 us
  other arithmetic: 114 us -> 0 us
  Pallas kernels: 0 us -> 39.2 us
  matrix products: 25.2 us -> 0 us
  between operations: 17.2 us -> 0.82 us
  starting transfers between devices: 0.98 us -> 12.8 us
    psum x6 -> x0, waiting for transfers between devices: 804 us -> none  [the longest x2 276 us: local(): lax.psum(jnp.dot(projected.T, projected, precision=highest), 'fsdp')]
    all_to_all x0 -> x7, blocking collectives: none -> 201 us  [the longest x4 131 us: all_sum(): terms = lax.all_to_all(x, axis, 0, 0)]
    another operation x18 -> x0, other arithmetic: 108 us -> none  [the longest x13 68.5 us: local(): factor = jnp.linalg.cholesky(gram_matrix)]
    pallas_call x0 -> x13, Pallas kernels: none -> 39.2 us  [call(): pl.pallas_call(kernel, out_shape=out_shape, compiler_params=pltpu.Compile...]
    psum x1 -> x0, blocking collectives: 24.8 us -> none  [local(): squares = lax.psum(jnp.sum(reflected * reflected, axis=0), 'tp')]
    dot_general x8 -> x0, matrix products: 21.9 us -> none  [the longest x2 7.03 us: local(): partial_proj = jnp.dot(combined, current, precision=highest)]
    all_to_all x0 -> x2, waiting for transfers between devices: none -> 16.3 us  [the longest x1 8.82 us: all_sum(): return lax.all_to_all(call(fold_kernel, shape(*x.shape), terms), axis, 0, 0)]
    unnamed x10 -> x30, local copies, waits for them, and re-layouts: 0.03 us -> 13.3 us
  transfers between devices with their start and end apart: 6 -> 2, of which waited for: 6 -> 2; matrix products, arithmetic and copies ran while one was open for 0% -> 0% of each run, Pallas kernels for 0% -> 5%
where the time goes in v1:
time: 285 us; the launch traced here: 284 us
  blocking collectives  201 us (71%)
  Pallas kernels  39.2 us (14%)
  waiting for transfers between devices  16.3 us (6%)
  local copies, waits for them, and re-layouts  13.3 us (5%)
  starting transfers between devices  12.8 us (4%)
    all_to_all x4, blocking collectives, all_sum(): terms = lax.all_to_all(x, axis, 0, 0)  131 us
    all_to_all x3, blocking collectives, all_sum(): return lax.all_to_all(call(fold_kernel, shape(*x.shape), terms), axis, 0, 0)  70.4 us
    pallas_call x13, Pallas kernels, call(): pl.pallas_call(kernel, out_shape=out_shape, compiler_params=pltpu.Compile...  39.2 us
    unnamed x30, local copies, waits for them, and re-layouts  13.3 us
    all_to_all x1, waiting for transfers between devices, all_sum(): return lax.all_to_all(call(fold_kernel, shape(*x.shape), terms), axis, 0, 0)  8.82 us
    all_to_all x1, waiting for transfers between devices, local(): squares = lax.all_to_all(squares, 'tp', 0, 0)  7.46 us
    all_to_all x1, starting transfers between devices, local(): squares = lax.all_to_all(squares, 'tp', 0, 0)  7.27 us
  transfers between devices with their start and end apart: 2, of which 2 were waited for; matrix products, arithmetic and copies ran while one was open for 0% of the time, Pallas kernels for 5%

profile of v1, /device:TPU:1, one launch (start us, length us, event | category | flops | bytes accessed | tf_op | source)
XLA Modules:
  0.0 283.8 jit_solution(10044541116117422106)
XLA Ops:
  0.6 0.0 copy-start.12
  0.6 1.7 copy.6.g_ref
  2.4 0.0 copy-done.12
  2.4 0.4 copy.7.m_ref
  2.8 0.0 copy-start.9
  2.8 1.0 copy-done.9
  3.8 1.3 shard_map.58
  5.1 47.8 %all_to_all.45.x_ref = f32[16,72,128]{2,1,0:T(8,128)S(1)} all-to-all(f32[16,72,128]{2,1,0:T(8,128)S(1)} %get-tuple-element.15), channel_id=1, replica_groups=mesh['fsdp'=32,'tp'=16] {'tp'}, dimensions={0} | all-to-all | bytes 1179648 | tf_op jit(solution)/shard_map/all_to_all | solution.py:103
  52.9 0.1 shard_map.59
  52.9 37.4 %all_to_all.46.p_ref = f32[16,72,128]{2,1,0:T(8,128)S(1)} all-to-all(f32[16,72,128]{2,1,0:T(8,128)S(1)} %shard_map.59), channel_id=1, replica_groups=mesh['fsdp'=32,'tp'=16] {'tp'}, dimensions={0} | all-to-all | bytes 1179648 | tf_op jit(solution)/shard_map/all_to_all | solution.py:104
  90.4 1.6 shard_map.60
  91.9 23.9 %all_to_all.47.x_ref = f32[32,40,128]{2,1,0:T(8,128)S(1)} all-to-all(f32[32,40,128]{2,1,0:T(8,128)S(1)} %bitcast.8), channel_id=1, replica_groups=mesh['fsdp'=32,'tp'=16] {'fsdp'}, dimensions={0} | all-to-all | bytes 1310720 | tf_op jit(solution)/shard_map/all_to_all | solution.py:103
  115.8 0.1 shard_map.61
  115.9 16.5 %all_to_all.48 = f32[32,40,128]{2,1,0:T(8,128)S(1)} all-to-all(f32[32,40,128]{2,1,0:T(8,128)S(1)} %shard_map.61), channel_id=1, replica_groups=mesh['fsdp'=32,'tp'=16] {'fsdp'}, dimensions={0} | all-to-all | bytes 1310720 | tf_op jit(solution)/shard_map/all_to_all | solution.py:104
  132.4 0.6 shard_map.62
  133.0 0.2 copy-done
  133.2 35.4 %all_to_all.49.x_ref = f32[16,72,128]{2,1,0:T(8,128)S(1)} all-to-all(f32[16,72,128]{2,1,0:T(8,128)S(1)} %shard_map.62), channel_id=1, replica_groups=mesh['fsdp'=32,'tp'=16] {'tp'}, dimensions={0} | all-to-all | bytes 1179648 | tf_op jit(solution)/shard_map/all_to_all | solution.py:103
  168.6 0.1 shard_map.63
  168.7 0.0 copy-start.2
  168.7 0.8 copy-done.2
  169.5 5.5 %all-to-all-start.5 = ((f32[16,72,128]{2,1,0:T(8,128)}), f32[16,72,128]{2,1,0:T(8,128)}, u32[]{:S(2)}, u32[]{:S(2)}) async-start(f32[16,72,128]{2,1,0:T(8,128)} %copy-done.2), calls=%async_computation.5 | async-start | bytes 1179648 | tf_op jit(solution)/shard_map/all_to_all | solution.py:104
  175.0 0.0 copy-start.1
  175.0 1.1 copy-done.1
  176.1 13.9 %shard_map.64.x_ref = f32[256,256]{1,0:T(8,128)S(1)} custom-call(f32[1280,128]{1,0:T(8,128)S(1)} %bitcast.7), custom_call_target="tpu_custom_call" | custom-call | flops 20000000000 | bytes 655360 | tf_op jit(solution)/shard_map/pallas_call | solution.py:50
  190.0 0.0 copy-start.10
  190.0 0.7 copy-done.10
  190.7 8.8 %all-to-all-done.5.p_ref = f32[16,72,128]{2,1,0:T(8,128)} async-done(((f32[16,72,128]{2,1,0:T(8,128)}), f32[16,72,128]{2,1,0:T(8,128)}, u32[]{:S(2)}, u32[]{:S(2)}) %all-to-all-start.5) | async-done | bytes 589856 | tf_op jit(solution)/shard_map/all_to_all | solution.py:104
  199.5 0.9 copy-done.11
  200.5 4.0 %shard_map.65 = (f32[576,256]{1,0:T(8,128)S(1)}, f32[1280,128]{1,0:T(8,128)S(1)}) custom-call(bf16[576,448]{1,0:T(8,128)(2,1)S(1)} %get-tuple-element.13.high_ref, bf16[576,448]{1,0:T(8,128)(2,1)S(1)} %get-tuple-element.14.low_ref, f32[16,72,128]{2,1,0:T(8,128)} %all-to-all-done.5.p_ref, f32[256,256]{1,0:T(8,128)S(1)} %copy-done.11), custom_call_target="tpu_custom_call" | custom-call | flops 396361728 | bytes 1884160 | tf_op jit(solution)/shard_map/pallas_call | solution.py:50
  204.5 23.9 %all_to_all.50.x_ref = f32[32,40,128]{2,1,0:T(8,128)S(1)} all-to-all(f32[32,40,128]{2,1,0:T(8,128)S(1)} %bitcast.9), channel_id=1, replica_groups=mesh['fsdp'=32,'tp'=16] {'fsdp'}, dimensions={0} | all-to-all | bytes 1310720 | tf_op jit(solution)/shard_map/all_to_all | solution.py:103
  228.4 0.1 shard_map.66
  228.5 16.5 %all_to_all.51 = f32[32,40,128]{2,1,0:T(8,128)S(1)} all-to-all(f32[32,40,128]{2,1,0:T(8,128)S(1)} %shard_map.66), channel_id=1, replica_groups=mesh['fsdp'=32,'tp'=16] {'fsdp'}, dimensions={0} | all-to-all | bytes 1310720 | tf_op jit(solution)/shard_map/all_to_all | solution.py:104
  245.0 13.9 %shard_map.67.x_ref = f32[256,256]{1,0:T(8,128)S(1)} custom-call(f32[1280,128]{1,0:T(8,128)S(1)} %bitcast.4), custom_call_target="tpu_custom_call" | custom-call | flops 20000000000 | bytes 655360 | tf_op jit(solution)/shard_map/pallas_call | solution.py:50
  258.9 1.3 shard_map.68
  260.2 0.8 copy-done.3
  261.0 0.8 copy-done.6
  261.8 7.3 %all-to-all-start.8 = ((f32[16,8,128]{2,1,0:T(8,128)}), f32[16,8,128]{2,1,0:T(8,128)}, u32[]{:S(2)}, u32[]{:S(2)}) async-start(f32[16,8,128]{2,1,0:T(8,128)} %get-tuple-element.20), calls=%async_computation.8 | async-start | bytes 131072 | tf_op jit(solution)/shard_map/all_to_all | solution.py:279
  269.1 0.0 copy-start.4
  269.1 1.1 copy-done.4
  270.1 1.0 copy-done.7
  271.2 0.7 shard_map.70
  271.8 0.0 copy-start.5
  271.8 0.0 copy-start.8
  271.8 1.4 copy.11
  273.2 7.5 %all-to-all-done.8.s_ref = f32[16,8,128]{2,1,0:T(8,128)} async-done(((f32[16,8,128]{2,1,0:T(8,128)}), f32[16,8,128]{2,1,0:T(8,128)}, u32[]{:S(2)}, u32[]{:S(2)}) %all-to-all-start.8) | async-done | bytes 65568 | tf_op jit(solution)/shard_map/all_to_all | solution.py:279
  280.7 0.0 copy-done.5
  280.7 1.7 shard_map.69
  282.4 1.4 copy.10
  (6 shorter events, 0.0 us)
Async XLA Ops:
  0.6 1.8 copy-start.12
  2.8 1.0 copy-start.9
  132.4 0.8 copy-start
  168.7 0.8 copy-start.2
  169.5 30.1 %all-to-all-start.5 = ((f32[16,72,128]{2,1,0:T(8,128)}), f32[16,72,128]{2,1,0:T(8,128)}, u32[]{:S(2)}, u32[]{:S(2)}) async-start(f32[16,72,128]{2,1,0:T(8,128)} %copy-done.2), calls=%async_computation.5 | async-start | bytes 1179648 | tf_op jit(solution)/shard_map/all_to_all | solution.py:104
  175.0 1.1 copy-start.1
  190.0 0.7 copy-start.10
  199.5 1.0 copy-start.11
  260.2 0.8 copy-start.3
  261.0 0.8 copy-start.6
  261.8 18.9 %all-to-all-start.8 = ((f32[16,8,128]{2,1,0:T(8,128)}), f32[16,8,128]{2,1,0:T(8,128)}, u32[]{:S(2)}, u32[]{:S(2)}) async-start(f32[16,8,128]{2,1,0:T(8,128)} %get-tuple-element.20), calls=%async_computation.8 | async-start | bytes 131072 | tf_op jit(solution)/shard_map/all_to_all | solution.py:279
  269.1 1.1 copy-start.4
  270.1 1.0 copy-start.7
  271.8 8.9 %copy-start.5 = (f32[576,256]{1,0:T(8,128)S(1)}, f32[576,256]{1,0:T(8,128)}, u32[]{:S(2)}) copy-start(f32[576,256]{1,0:T(8,128)} %copy-done.3) | copy-start | bytes 1769476
  271.8 8.9 %copy-start.8 = (f32[448,256]{1,0:T(8,128)S(1)}, f32[448,256]{1,0:T(8,128)}, u32[]{:S(2)}) copy-start(f32[448,256]{1,0:T(8,128)} %copy-done.6) | copy-start | bytes 1376260

commit v2 on v1

--- a/solution.py
+++ b/solution.py
@@ -24,7 +24,7 @@
 F32 = jnp.float32
 BF16 = jnp.bfloat16
 HIGHEST = lax.Precision.HIGHEST
-PANEL = 4
+PANEL = 8
 
 NN = (((1,), (0,)), ((), ()))
 NT = (((1,), (1,)), ((), ()))
@@ -45,12 +45,12 @@
     return lax.dot_general(a, b, dims, precision=HIGHEST, preferred_element_type=F32)
 
 
-def call(kernel, out_shape, *args, flops=0, **kw):
+def call(kernel, out_shape, *args, flops=0, vmem=48, **kw):
     n_bytes = sum(x.size * x.dtype.itemsize for x in args)
     return pl.pallas_call(
         kernel,
         out_shape=out_shape,
-        compiler_params=pltpu.CompilerParams(vmem_limit_bytes=48 * 2**20),
+        compiler_params=pltpu.CompilerParams(vmem_limit_bytes=vmem * 2**20),
         cost_estimate=pl.CostEstimate(flops=flops, bytes_accessed=n_bytes, transcendentals=0),
         **kw,
     )(*args)
@@ -60,10 +60,11 @@
     return jax.ShapeDtypeStruct(dims, dtype)
 
 
-def put_bands(ref, value):
-    for i in range(value.shape[0] // BAND):
-        for h in range(2):
-            ref[2 * i + h] = value[i * BAND : (i + 1) * BAND, h * HALF : (h + 1) * HALF]
+def put_halves(own_ref, other_ref, value):
+    left, right = value[:, :HALF], value[:, HALF:]
+    even = lax.rem(lax.axis_index("tp"), 2) == 0
+    own_ref[...] = jnp.where(even, left, right)
+    other_ref[...] = jnp.where(even, right, left)
 
 
 def get_bands(ref):
@@ -71,27 +72,44 @@
     return jnp.concatenate([x.reshape(ROWS, HALF) for x in halves], axis=1)
 
 
-def first_kernel(g_ref, m_ref, b_ref, high_ref, low_ref, out_ref):
+def first_kernel(g_ref, m_ref, b_ref, high_ref, low_ref, own_ref, other_ref, total_ref):
+    step = pl.program_id(0)
     high, low = split(m_ref[...] + g_ref[...])
     high_ref[...] = high
     low_ref[...] = low
-    put_bands(out_ref, dot3((high, low), split(b_ref[...]), NN))
+    term = dot3((high, low), split(b_ref[...]), TN)
+
+    @pl.when(step == 0)
+    def _():
+        total_ref[...] = term
+
+    @pl.when(step > 0)
+    def _():
+        total_ref[...] += term
+
+    @pl.when(step == pl.num_programs(0) - 1)
+    def _():
+        put_halves(own_ref, other_ref, total_ref[...])
 
 
 def first(g, m, b):
     n = 4
-    rows = ROWS // n
-    block = pl.BlockSpec((rows, COLS), lambda i: (i, 0))
+    wide = shape(COLS, ROWS, dtype=BF16)
+    half = shape(ROWS, HALF)
+    block = pl.BlockSpec((COLS // n, ROWS), lambda i: (i, 0))
+    whole = pl.BlockSpec((ROWS, HALF), lambda i: (0, 0))
     return call(
         first_kernel,
-        (shape(ROWS, COLS, dtype=BF16), shape(ROWS, COLS, dtype=BF16), shape(TP, BAND, HALF)),
+        (wide, wide, half, half),
         g,
         m,
         b,
         flops=6 * ROWS * COLS * RANK,
+        vmem=60,
         grid=(n,),
-        in_specs=[block, block, pl.BlockSpec((COLS, RANK), lambda i: (0, 0))],
-        out_specs=[block, block, pl.BlockSpec((TP // n, BAND, HALF), lambda i: (i, 0, 0))],
+        in_specs=[block, block, pl.BlockSpec((COLS // n, RANK), lambda i: (i, 0))],
+        out_specs=[block, block, whole, whole],
+        scratch_shapes=[pltpu.VMEM((ROWS, RANK), F32)],
     )
 
 
@@ -102,6 +120,20 @@
 def all_sum(x, axis):
     terms = lax.all_to_all(x, axis, 0, 0)
     return lax.all_to_all(call(fold_kernel, shape(*x.shape), terms), axis, 0, 0)
+
+
+def band_kernel(x_ref, out_ref):
+    out_ref[...] = jnp.sum(x_ref[...], axis=0)
+
+
+def tp_sum(own, other, beside=None):
+    own = own + lax.ppermute(other, "tp", [(i, i ^ 1) for i in range(TP)])
+    places = [list(range(i, TP, 2)) for i in range(2)]
+    terms = lax.all_to_all(own.reshape(TP // 2, BAND, HALF), "tp", 0, 0, axis_index_groups=places)
+    band = call(band_kernel, shape(BAND, HALF), terms)
+    if beside is not None:
+        band, beside = lax.optimization_barrier((band, beside))
+    return lax.all_gather(band, "tp"), beside
 
 
 def put_reflected(ref, c, p):
@@ -118,25 +150,27 @@
 
 def reflect_kernel(high_ref, low_ref, p_ref, out_ref):
     p = get_bands(p_ref)
-    put_reflected(out_ref, dot3((high_ref[...], low_ref[...]), split(p), TN), p)
+    put_reflected(out_ref, dot3((high_ref[...], low_ref[...]), split(p), NN), p)
 
 
 def reflect(high, low, p):
     return call(reflect_kernel, shape(FSDP * SHARE, HALF), high, low, p, flops=6 * ROWS * COLS * RANK)
 
 
-def project_kernel(high_ref, low_ref, c_ref, out_ref):
-    put_bands(out_ref, dot3((high_ref[...], low_ref[...]), split(get_reflected(c_ref)), NN))
+def project_kernel(high_ref, low_ref, c_ref, own_ref, other_ref):
+    c = split(get_reflected(c_ref))
+    put_halves(own_ref, other_ref, dot3((high_ref[...], low_ref[...]), c, TN))
 
 
 def project(high, low, c):
-    return call(project_kernel, shape(TP, BAND, HALF), high, low, c, flops=6 * ROWS * COLS * RANK)
+    half = shape(ROWS, HALF)
+    return call(project_kernel, (half, half), high, low, c, flops=6 * ROWS * COLS * RANK)
 
 
 def second_reflect_kernel(high_ref, low_ref, p_ref, x_ref, p_out_ref, out_ref):
-    p = dot6(get_bands(p_ref), x_ref[...], NT)
+    p = dot3(split(get_bands(p_ref)), split(x_ref[...]), NT)
     p_out_ref[...] = p
-    put_reflected(out_ref, dot3((high_ref[...], low_ref[...]), split(p), TN), p)
+    put_reflected(out_ref, dot3((high_ref[...], low_ref[...]), split(p), NN), p)
 
 
 def second_reflect(high, low, p, x):
@@ -161,20 +195,18 @@
     e = [jnp.where(col_at == row_at + 8 * v, 1.0, 0.0).astype(F32) for v in range(n)]
     out = []
     for k0 in range(0, HALF, PANEL):
-        v0, s0 = k0 // 8, k0 % 8
-        last = k0 + PANEL >= 8 * (v0 + 1)
-        cols = {v: [lanes(a[v], k0 + j) for j in range(PANEL)] for v in range(v0, n)}
-        rows = [sublanes(a[v0], s0 + j) for j in range(PANEL)]
-        units = [sublanes(e[v0], s0 + j) for j in range(PANEL)]
-        d = [[sublanes(cols[v0][j], s0 + i) for j in range(i + 1)] for i in range(PANEL)]
+        place = [divmod(k0 + j, 8) for j in range(PANEL)]
+        cols = {v: [lanes(a[v], k0 + j) for j in range(PANEL)] for v in range(k0 // 8, n)}
+        rows = [sublanes(a[v], k) for v, k in place]
+        units = [sublanes(e[v], k) for v, k in place]
+        d = [[sublanes(cols[v][j], k) for j in range(i + 1)] for i, (v, k) in enumerate(place)]
         factor = [[None] * PANEL for _ in range(PANEL)]
         inverse = [None] * PANEL
         for j in range(PANEL):
             t = d[j][j]
             for k in range(j):
                 t = t - factor[j][k] * factor[j][k]
-            r = lax.rsqrt(t)
-            inverse[j] = r * (1.5 - 0.5 * t * (r * r))
+            inverse[j] = lax.rsqrt(t)
             for i in range(j + 1, PANEL):
                 t = d[i][j]
                 for k in range(j):
@@ -192,7 +224,7 @@
 
         rows, units = solve(rows), solve(units)
         out += [u[:1] for u in units]
-        for v in range(v0 + 1 if last else v0, n):
+        for v in range((k0 + PANEL) // 8, n):
             c = solve(cols[v])
             for j in range(PANEL):
                 a[v] = a[v] - c[j] * rows[j]
@@ -251,7 +283,7 @@
 
 
 def momentum_kernel(g_ref, m_ref, q_ref, r_ref, out_ref):
-    product = dot3(split(q_ref[...]), split(r_ref[...]), NT)
+    product = dot3(split(r_ref[...]), split(q_ref[...]), NT)
     out_ref[...] = (m_ref[...] + g_ref[...]) - (1.0 - decay_rate) * product
 
 
@@ -261,28 +293,28 @@
     scale = jnp.concatenate([scale[:1], scale[4:5]], axis=1)
     d = r_ref[...] * scale
     d_ref[...] = d
-    out_ref[...] = math.sqrt(M_ROWS / RANK) * dot3(split(q_ref[...]), split(d), NT)
+    out_ref[...] = math.sqrt(M_ROWS / RANK) * dot3(split(d), split(q_ref[...]), NT)
 
 
 def local(gradient, momentum, start_basis):
-    high, low, p = first(gradient, momentum, start_basis)
-    p = all_sum(p, "tp")
+    gradient, momentum = gradient.T, momentum.T
+    high, low, *p = first(gradient, momentum, start_basis)
+    p, _ = tp_sum(*p)
     c = reflect(high, low, p)
     c = all_sum(c.reshape(FSDP, SHARE, HALF), "fsdp").reshape(FSDP * SHARE, HALF)
     p = project(high, low, c)
-    x = inverse_factor(c)
-    p = all_sum(p, "tp")
+    p, x = tp_sum(*p, inverse_factor(c))
     p, c = second_reflect(high, low, p, x)
     c = all_sum(c.reshape(FSDP, SHARE, HALF), "fsdp").reshape(FSDP * SHARE, HALF)
     x = inverse_factor(c)
     q, r, squares = basis(p, c, x)
     squares = lax.all_to_all(squares, "tp", 0, 0)
     flops = 6 * ROWS * COLS * RANK
-    new_momentum = call(momentum_kernel, shape(ROWS, COLS), gradient, momentum, q, r, flops=flops)
+    new_momentum = call(momentum_kernel, shape(COLS, ROWS), gradient, momentum, q, r, flops=flops)
     update, directions = call(
-        update_kernel, (shape(ROWS, COLS), shape(COLS, RANK)), q, r, squares, flops=flops
-    )
-    return (update, new_momentum, directions)
+        update_kernel, (shape(COLS, ROWS), shape(COLS, RANK)), q, r, squares, flops=flops
+    )
+    return (update.T, new_momentum.T, directions)
 
 
 def solution(mesh):

time: 285 us -> 259 us (0.909)
  blocking collectives: 201 us -> 175 us
  local copies, waits for them, and re-layouts: 13.3 us -> 0.02 us
  waiting for transfers between devices: 16.3 us -> 28.5 us
  Pallas kernels: 39.2 us -> 33.9 us
  starting transfers between devices: 12.8 us -> 18.1 us
    all_to_all x4 -> x2, blocking collectives: 131 us -> 52.2 us  [all_sum(): terms = lax.all_to_all(x, axis, 0, 0)]
    all_gather x0 -> x2, blocking collectives: none -> 56.3 us  [tp_sum(): return (lax.all_gather(band, 'tp'), beside)]
    all_to_all x3 -> x2, blocking collectives: 70.4 us -> 33 us  [all_sum(): return lax.all_to_all(call(fold_kernel, shape(*x.shape), terms), axis, 0, 0)]
    all_to_all x0 -> x1, blocking collectives: none -> 33.7 us  [tp_sum(): lax.all_to_all(own.reshape(TP // 2, BAND, HALF), 'tp', 0, 0, axis_index_g...]
    unnamed x30 -> x8, local copies, waits for them, and re-layouts: 13.3 us -> 0.02 us
    ppermute x0 -> x2, waiting for transfers between devices: none -> 11 us  [tp_sum(): own = own + lax.ppermute(other, 'tp', [(i, i ^ 1) for i in range(TP)])]
    ppermute x0 -> x2, starting transfers between devices: none -> 7.57 us  [tp_sum(): own = own + lax.ppermute(other, 'tp', [(i, i ^ 1) for i in range(TP)])]
    pallas_call x13, Pallas kernels: 39.2 us -> 33.9 us  [call(): pl.pallas_call(kernel, out_shape=out_shape, compiler_params=pltpu.Compile...]
  transfers between devices with their start and end apart: 2 -> 4, of which waited for: 2 -> 4; matrix products, arithmetic and copies ran while one was open for 0% -> 0% of each run, Pallas kernels for 5% -> 4%
where the time goes in v2:
time: 259 us; the launch traced here: 258 us
  blocking collectives  175 us (68%)
  Pallas kernels  33.9 us (13%)
  waiting for transfers between devices  28.5 us (11%)
  starting transfers between devices  18.1 us (7%)
    all_gather x2, blocking collectives, tp_sum(): return (lax.all_gather(band, 'tp'), beside)  56.3 us
    all_to_all x2, blocking collectives, all_sum(): terms = lax.all_to_all(x, axis, 0, 0)  52.2 us
    pallas_call x13, Pallas kernels, call(): pl.pallas_call(kernel, out_shape=out_shape, compiler_params=pltpu.Compile...  33.9 us
    all_to_all x1, blocking collectives, tp_sum(): lax.all_to_all(own.reshape(TP // 2, BAND, HALF), 'tp', 0, 0, axis_index_g...  33.7 us
    all_to_all x2, blocking collectives, all_sum(): return lax.all_to_all(call(fold_kernel, shape(*x.shape), terms), axis, 0, 0)  33 us
    ppermute x2, waiting for transfers between devices, tp_sum(): own = own + lax.ppermute(other, 'tp', [(i, i ^ 1) for i in range(TP)])  11 us
    all_to_all x1, waiting for transfers between devices, local(): squares = lax.all_to_all(squares, 'tp', 0, 0)  9.84 us
    all_to_all x1, waiting for transfers between devices, tp_sum(): lax.all_to_all(own.reshape(TP // 2, BAND, HALF), 'tp', 0, 0, axis_index_g...  7.68 us
  transfers between devices with their start and end apart: 4, of which 4 were waited for; matrix products, arithmetic and copies ran while one was open for 0% of the time, Pallas kernels for 4%

profile of v2, /device:TPU:1, one launch (start us, length us, event | category | flops | bytes accessed | tf_op | source)
XLA Modules:
  0.0 258.2 jit_solution(16249518717349098994)
XLA Ops:
  0.6 4.8 %shard_map.58 = (bf16[448,576]{1,0:T(8,128)(2,1)}, bf16[448,576]{1,0:T(8,128)(2,1)}, f32[576,128]{1,0:T(8,128)}, f32[576,128]{1,0:T(8,128)}) custom-call(f32[448,576]{1,0:T(8,128)} %bitcast.12, f32[448,576]{1,0:T(8,128)} %bitcast.14, f32[448,256]{1,0:T(8,128)} %b_ref.1), custom_call_target="tpu_custom_call" | custom-call | flops 396361728 | bytes 2523136 | tf_op jit(solution)/shard_map/pallas_call | solution.py:50
  5.4 4.4 %collective-permute-start = (f32[576,128]{1,0:T(8,128)}, f32[576,128]{1,0:T(8,128)S(1)}, u32[]{:S(2)}, u32[]{:S(2)}) collective-permute-start(f32[576,128]{1,0:T(8,128)} %get-tuple-element.21), channel_id=1, source_target_pairs={{0,1},{1,0},{2,3},{3,2},{4,5},{5,4},{6,7},{7,6},{8,9},{9,8},{10,11... | collective-permute-start | bytes 884744 | tf_op jit(solution)/shard_map/ppermute | solution.py:130
  9.8 4.3 %collective-permute-done = f32[576,128]{1,0:T(8,128)S(1)} collective-permute-done((f32[576,128]{1,0:T(8,128)}, f32[576,128]{1,0:T(8,128)S(1)}, u32[]{:S(2)}, u32[]{:S(2)}) %collective-permute-start) | collective-permute-done | bytes 294944 | tf_op jit(solution)/shard_map/ppermute | solution.py:130
  14.1 0.0 copy-start
  14.1 0.0 copy-start.1
  14.1 1.1 add.6
  15.2 33.7 %all_to_all.35.x_ref = f32[8,72,128]{2,1,0:T(8,128)S(1)} all-to-all(f32[8,72,128]{2,1,0:T(8,128)S(1)} %bitcast.24), channel_id=1, replica_groups={{0,2,4,6,8,10,12,14},{1,3,5,7,9,11,13,15},{16,18,20,22,24,26,28,30},{17..., dimensions={0} | all-to-all | bytes 589824 | tf_op jit(solution)/shard_map/all_to_all | solution.py:132
  48.9 28.7 %all-gather = f32[1152,128]{1,0:T(8,128)S(1)} all-gather(f32[72,128]{1,0:T(8,128)S(1)} %shard_map.59), channel_id=2, replica_groups=mesh['fsdp'=32,'tp'=16] {'tp'}, dimensions={0}, use_global_device_ids=true | all-gather | bytes 626688 | tf_op jit(solution)/shard_map/all_gather | solution.py:136
  77.6 0.0 copy-done
  77.6 0.0 copy-done.1
  77.6 1.5 shard_map.60
  79.1 28.2 %all_to_all.36.x_ref = f32[32,40,128]{2,1,0:T(8,128)S(1)} all-to-all(f32[32,40,128]{2,1,0:T(8,128)S(1)} %bitcast.18), channel_id=1, replica_groups=mesh['fsdp'=32,'tp'=16] {'fsdp'}, dimensions={0} | all-to-all | bytes 1310720 | tf_op jit(solution)/shard_map/all_to_all | solution.py:121
  107.3 0.1 shard_map.61
  107.4 16.5 %all_to_all.37 = f32[32,40,128]{2,1,0:T(8,128)S(1)} all-to-all(f32[32,40,128]{2,1,0:T(8,128)S(1)} %shard_map.61), channel_id=1, replica_groups=mesh['fsdp'=32,'tp'=16] {'fsdp'}, dimensions={0} | all-to-all | bytes 1310720 | tf_op jit(solution)/shard_map/all_to_all | solution.py:122
  123.8 0.7 shard_map.62
  124.5 3.2 %collective-permute-start.1 = (f32[576,128]{1,0:T(8,128)S(1)}, f32[576,128]{1,0:T(8,128)S(1)}, u32[]{:S(2)}, u32[]{:S(2)}) collective-permute-start(f32[576,128]{1,0:T(8,128)S(1)} %get-tuple-element.23), channel_id=1, source_target_pairs={{0,1},{1,0},{2,3},{3,2},{4,5},{5,4},{6,7},{7,6},{8,9},{9,8},{10,11... | collective-permute-start | bytes 884744 | tf_op jit(solution)/shard_map/ppermute | solution.py:130
  127.7 6.7 %collective-permute-done.1 = f32[576,128]{1,0:T(8,128)S(1)} collective-permute-done((f32[576,128]{1,0:T(8,128)S(1)}, f32[576,128]{1,0:T(8,128)S(1)}, u32[]{:S(2)}, u32[]{:S(2)}) %collective-permute-start.1) | collective-permute-done | bytes 294944 | tf_op jit(solution)/shard_map/ppermute | solution.py:130
  134.5 0.7 add.7
  135.2 5.4 %all-to-all-start.3 = ((f32[8,72,128]{2,1,0:T(8,128)}), f32[8,72,128]{2,1,0:T(8,128)S(1)}, u32[]{:S(2)}, u32[]{:S(2)}) async-start(f32[8,72,128]{2,1,0:T(8,128)} %bitcast.6), calls=%async_computation.3 | async-start | bytes 589824 | tf_op jit(solution)/shard_map/all_to_all | solution.py:132
  140.6 9.8 %shard_map.64.x_ref = f32[256,256]{1,0:T(8,128)S(1)} custom-call(f32[1280,128]{1,0:T(8,128)S(1)} %bitcast.17), custom_call_target="tpu_custom_call" | custom-call | flops 20000000000 | bytes 655360 | tf_op jit(solution)/shard_map/pallas_call | solution.py:50
  150.4 7.7 %all-to-all-done.3.x_ref = f32[8,72,128]{2,1,0:T(8,128)S(1)} async-done(((f32[8,72,128]{2,1,0:T(8,128)}), f32[8,72,128]{2,1,0:T(8,128)S(1)}, u32[]{:S(2)}, u32[]{:S(2)}) %all-to-all-start.3) | async-done | bytes 294944 | tf_op jit(solution)/shard_map/all_to_all | solution.py:132
  158.1 27.6 %all-gather.1 = f32[1152,128]{1,0:T(8,128)S(1)} all-gather(f32[72,128]{1,0:T(8,128)S(1)} %shard_map.63), channel_id=3, replica_groups=mesh['fsdp'=32,'tp'=16] {'tp'}, dimensions={0}, use_global_device_ids=true | all-gather | bytes 626688 | tf_op jit(solution)/shard_map/all_gather | solution.py:136
  185.7 2.3 shard_map.65
  188.0 24.0 %all_to_all.38.x_ref = f32[32,40,128]{2,1,0:T(8,128)S(1)} all-to-all(f32[32,40,128]{2,1,0:T(8,128)S(1)} %bitcast.23), channel_id=1, replica_groups=mesh['fsdp'=32,'tp'=16] {'fsdp'}, dimensions={0} | all-to-all | bytes 1310720 | tf_op jit(solution)/shard_map/all_to_all | solution.py:121
  212.1 0.1 shard_map.66
  212.1 16.5 %all_to_all.39 = f32[32,40,128]{2,1,0:T(8,128)S(1)} all-to-all(f32[32,40,128]{2,1,0:T(8,128)S(1)} %shard_map.66), channel_id=1, replica_groups=mesh['fsdp'=32,'tp'=16] {'fsdp'}, dimensions={0} | all-to-all | bytes 1310720 | tf_op jit(solution)/shard_map/all_to_all | solution.py:122
  228.6 0.0 copy-start.3
  228.6 9.8 %shard_map.67.x_ref = f32[256,256]{1,0:T(8,128)S(1)} custom-call(f32[1280,128]{1,0:T(8,128)S(1)} %bitcast.19), custom_call_target="tpu_custom_call" | custom-call | flops 20000000000 | bytes 655360 | tf_op jit(solution)/shard_map/pallas_call | solution.py:50
  238.5 0.0 copy-start.2
  238.5 1.3 shard_map.68
  239.8 5.1 %all-to-all-start.6 = ((f32[16,8,128]{2,1,0:T(8,128)}), f32[16,8,128]{2,1,0:T(8,128)S(1)}, u32[]{:S(2)}, u32[]{:S(2)}) async-start(f32[16,8,128]{2,1,0:T(8,128)} %get-tuple-element.30), calls=%async_computation.6 | async-start | bytes 131072 | tf_op jit(solution)/shard_map/all_to_all | solution.py:311
  244.9 0.0 copy-done.3
  245.0 0.0 copy-done.2
  245.0 1.7 shard_map.70
  246.7 9.8 %all-to-all-done.6.s_ref = f32[16,8,128]{2,1,0:T(8,128)S(1)} async-done(((f32[16,8,128]{2,1,0:T(8,128)}), f32[16,8,128]{2,1,0:T(8,128)S(1)}, u32[]{:S(2)}, u32[]{:S(2)}) %all-to-all-start.6) | async-done | bytes 65568 | tf_op jit(solution)/shard_map/all_to_all | solution.py:311
  256.5 1.7 shard_map.69
  (2 shorter events, 0.0 us)
Async XLA Ops:
  5.4 8.7 %collective-permute-start = (f32[576,128]{1,0:T(8,128)}, f32[576,128]{1,0:T(8,128)S(1)}, u32[]{:S(2)}, u32[]{:S(2)}) collective-permute-start(f32[576,128]{1,0:T(8,128)} %get-tuple-element.21), channel_id=1, source_target_pairs={{0,1},{1,0},{2,3},{3,2},{4,5},{5,4},{6,7},{7,6},{8,9},{9,8},{10,11... | collective-permute-start | bytes 884744 | tf_op jit(solution)/shard_map/ppermute | solution.py:130
  14.1 63.5 %copy-start = (bf16[448,576]{1,0:T(8,128)(2,1)S(1)}, bf16[448,576]{1,0:T(8,128)(2,1)}, u32[]{:S(2)}) copy-start(bf16[448,576]{1,0:T(8,128)(2,1)} %get-tuple-element.18.high_ref) | copy-start | bytes 1548292
  14.1 63.5 %copy-start.1 = (bf16[448,576]{1,0:T(8,128)(2,1)S(1)}, bf16[448,576]{1,0:T(8,128)(2,1)}, u32[]{:S(2)}) copy-start(bf16[448,576]{1,0:T(8,128)(2,1)} %get-tuple-element.19.low_ref) | copy-start | bytes 1548292
  124.5 9.9 %collective-permute-start.1 = (f32[576,128]{1,0:T(8,128)S(1)}, f32[576,128]{1,0:T(8,128)S(1)}, u32[]{:S(2)}, u32[]{:S(2)}) collective-permute-start(f32[576,128]{1,0:T(8,128)S(1)} %get-tuple-element.23), channel_id=1, source_target_pairs={{0,1},{1,0},{2,3},{3,2},{4,5},{5,4},{6,7},{7,6},{8,9},{9,8},{10,11... | collective-permute-start | bytes 884744 | tf_op jit(solution)/shard_map/ppermute | solution.py:130
  135.2 22.9 %all-to-all-start.3 = ((f32[8,72,128]{2,1,0:T(8,128)}), f32[8,72,128]{2,1,0:T(8,128)S(1)}, u32[]{:S(2)}, u32[]{:S(2)}) async-start(f32[8,72,128]{2,1,0:T(8,128)} %bitcast.6), calls=%async_computation.3 | async-start | bytes 589824 | tf_op jit(solution)/shard_map/all_to_all | solution.py:132
  228.6 16.3 %copy-start.3 = (f32[576,448]{0,1:T(8,128)S(1)}, f32[576,448]{0,1:T(8,128)}, u32[]{:S(2)}) copy-start(f32[576,448]{0,1:T(8,128)} %param.4) | copy-start | bytes 3096580
  238.5 6.5 %copy-start.2 = (f32[576,448]{0,1:T(8,128)S(1)}, f32[576,448]{0,1:T(8,128)}, u32[]{:S(2)}) copy-start(f32[576,448]{0,1:T(8,128)} %param.3) | copy-start | bytes 3096580
  239.8 16.7 %all-to-all-start.6 = ((f32[16,8,128]{2,1,0:T(8,128)}), f32[16,8,128]{2,1,0:T(8,128)S(1)}, u32[]{:S(2)}, u32[]{:S(2)}) async-start(f32[16,8,128]{2,1,0:T(8,128)} %get-tuple-element.30), calls=%async_computation.6 | async-start | bytes 131072 | tf_op jit(solution)/shard_map/all_to_all | solution.py:311

commit v3 on v2

--- a/solution.py
+++ b/solution.py
@@ -25,6 +25,7 @@
 BF16 = jnp.bfloat16
 HIGHEST = lax.Precision.HIGHEST
 PANEL = 8
+RUN = 4
 
 NN = (((1,), (0,)), ((), ()))
 NT = (((1,), (1,)), ((), ()))
@@ -60,11 +61,11 @@
     return jax.ShapeDtypeStruct(dims, dtype)
 
 
-def put_halves(own_ref, other_ref, value):
-    left, right = value[:, :HALF], value[:, HALF:]
-    even = lax.rem(lax.axis_index("tp"), 2) == 0
-    own_ref[...] = jnp.where(even, left, right)
-    other_ref[...] = jnp.where(even, right, left)
+def put_bands(ref, value):
+    for i in range(ROWS // BAND):
+        for h in range(2):
+            run, place = divmod(2 * i + h, RUN)
+            ref[place * RUN + run] = value[i * BAND : (i + 1) * BAND, h * HALF : (h + 1) * HALF]
 
 
 def get_bands(ref):
@@ -72,44 +73,17 @@
     return jnp.concatenate([x.reshape(ROWS, HALF) for x in halves], axis=1)
 
 
-def first_kernel(g_ref, m_ref, b_ref, high_ref, low_ref, own_ref, other_ref, total_ref):
-    step = pl.program_id(0)
+def first_kernel(g_ref, m_ref, b_ref, high_ref, low_ref, out_ref):
     high, low = split(m_ref[...] + g_ref[...])
     high_ref[...] = high
     low_ref[...] = low
-    term = dot3((high, low), split(b_ref[...]), TN)
-
-    @pl.when(step == 0)
-    def _():
-        total_ref[...] = term
-
-    @pl.when(step > 0)
-    def _():
-        total_ref[...] += term
-
-    @pl.when(step == pl.num_programs(0) - 1)
-    def _():
-        put_halves(own_ref, other_ref, total_ref[...])
+    put_bands(out_ref, dot3((high, low), split(b_ref[...]), TN))
 
 
 def first(g, m, b):
-    n = 4
     wide = shape(COLS, ROWS, dtype=BF16)
-    half = shape(ROWS, HALF)
-    block = pl.BlockSpec((COLS // n, ROWS), lambda i: (i, 0))
-    whole = pl.BlockSpec((ROWS, HALF), lambda i: (0, 0))
-    return call(
-        first_kernel,
-        (wide, wide, half, half),
-        g,
-        m,
-        b,
-        flops=6 * ROWS * COLS * RANK,
-        vmem=60,
-        grid=(n,),
-        in_specs=[block, block, pl.BlockSpec((COLS // n, RANK), lambda i: (i, 0))],
-        out_specs=[block, block, whole, whole],
-        scratch_shapes=[pltpu.VMEM((ROWS, RANK), F32)],
+    return call(
+        first_kernel, (wide, wide, shape(TP, BAND, HALF)), g, m, b, flops=6 * ROWS * COLS * RANK
     )
 
 
@@ -122,15 +96,17 @@
     return lax.all_to_all(call(fold_kernel, shape(*x.shape), terms), axis, 0, 0)
 
 
-def band_kernel(x_ref, out_ref):
+def add_kernel(x_ref, out_ref):
     out_ref[...] = jnp.sum(x_ref[...], axis=0)
 
 
-def tp_sum(own, other, beside=None):
-    own = own + lax.ppermute(other, "tp", [(i, i ^ 1) for i in range(TP)])
-    places = [list(range(i, TP, 2)) for i in range(2)]
-    terms = lax.all_to_all(own.reshape(TP // 2, BAND, HALF), "tp", 0, 0, axis_index_groups=places)
-    band = call(band_kernel, shape(BAND, HALF), terms)
+def tp_sum(x, beside=None):
+    near = [list(range(i, i + RUN)) for i in range(0, TP, RUN)]
+    far = [list(range(i, TP, RUN)) for i in range(RUN)]
+    x = lax.all_to_all(x.reshape(RUN, RUN * BAND, HALF), "tp", 0, 0, axis_index_groups=near)
+    x = call(add_kernel, shape(RUN * BAND, HALF), x).reshape(RUN, BAND, HALF)
+    x = lax.all_to_all(x, "tp", 0, 0, axis_index_groups=far)
+    band = call(add_kernel, shape(BAND, HALF), x)
     if beside is not None:
         band, beside = lax.optimization_barrier((band, beside))
     return lax.all_gather(band, "tp"), beside
@@ -157,14 +133,12 @@
     return call(reflect_kernel, shape(FSDP * SHARE, HALF), high, low, p, flops=6 * ROWS * COLS * RANK)
 
 
-def project_kernel(high_ref, low_ref, c_ref, own_ref, other_ref):
-    c = split(get_reflected(c_ref))
-    put_halves(own_ref, other_ref, dot3((high_ref[...], low_ref[...]), c, TN))
+def project_kernel(high_ref, low_ref, c_ref, out_ref):
+    put_bands(out_ref, dot3((high_ref[...], low_ref[...]), split(get_reflected(c_ref)), TN))
 
 
 def project(high, low, c):
-    half = shape(ROWS, HALF)
-    return call(project_kernel, (half, half), high, low, c, flops=6 * ROWS * COLS * RANK)
+    return call(project_kernel, shape(TP, BAND, HALF), high, low, c, flops=6 * ROWS * COLS * RANK)
 
 
 def second_reflect_kernel(high_ref, low_ref, p_ref, x_ref, p_out_ref, out_ref):
@@ -260,10 +234,8 @@
     )
 
 
-def basis_kernel(p_ref, c_ref, x_ref, q_ref, r_ref, s_ref):
-    x = split(x_ref[...])
-    q_ref[...] = dot3(split(p_ref[...]), x, NT)
-    r = dot3(split(get_reflected(c_ref)), x, NT)
+def right_kernel(c_ref, x_ref, r_ref, s_ref):
+    r = dot3(split(get_reflected(c_ref)), split(x_ref[...]), NT)
     r_ref[...] = r
     squares = jnp.sum(r * r, axis=0, keepdims=True)
     for h in range(2):
@@ -271,15 +243,14 @@
         s_ref[:, 4 * h : 4 * h + 4, :] = jnp.broadcast_to(half[None], (TP, 4, HALF))
 
 
-def basis(p, c, x):
-    return call(
-        basis_kernel,
-        (shape(ROWS, RANK), shape(COLS, RANK), shape(TP, 8, HALF)),
-        p,
-        c,
-        x,
-        flops=6 * (ROWS + COLS) * RANK * RANK,
-    )
+def right(c, x):
+    return call(
+        right_kernel, (shape(COLS, RANK), shape(TP, 8, HALF)), c, x, flops=6 * COLS * RANK * RANK
+    )
+
+
+def left_kernel(p_ref, x_ref, q_ref):
+    q_ref[...] = dot3(split(p_ref[...]), split(x_ref[...]), NT)
 
 
 def momentum_kernel(g_ref, m_ref, q_ref, r_ref, out_ref):
@@ -298,17 +269,18 @@
 
 def local(gradient, momentum, start_basis):
     gradient, momentum = gradient.T, momentum.T
-    high, low, *p = first(gradient, momentum, start_basis)
-    p, _ = tp_sum(*p)
+    high, low, p = first(gradient, momentum, start_basis)
+    p, _ = tp_sum(p)
     c = reflect(high, low, p)
     c = all_sum(c.reshape(FSDP, SHARE, HALF), "fsdp").reshape(FSDP * SHARE, HALF)
     p = project(high, low, c)
-    p, x = tp_sum(*p, inverse_factor(c))
+    p, x = tp_sum(p, inverse_factor(c))
     p, c = second_reflect(high, low, p, x)
     c = all_sum(c.reshape(FSDP, SHARE, HALF), "fsdp").reshape(FSDP * SHARE, HALF)
     x = inverse_factor(c)
-    q, r, squares = basis(p, c, x)
+    r, squares = right(c, x)
     squares = lax.all_to_all(squares, "tp", 0, 0)
+    q = call(left_kernel, shape(ROWS, RANK), p, x, flops=6 * ROWS * RANK * RANK)
     flops = 6 * ROWS * COLS * RANK
     new_momentum = call(momentum_kernel, shape(COLS, ROWS), gradient, momentum, q, r, flops=flops)
     update, directions = call(

time: 259 us -> 262 us (1.012)
  blocking collectives: 175 us -> 203 us
  waiting for transfers between devices: 28.5 us -> 9.6 us
  starting transfers between devices: 18.1 us -> 10.7 us
  local copies, waits for them, and re-layouts: 0.02 us -> 6.39 us
  Pallas kernels: 33.9 us -> 30.7 us
    all_to_all x1 -> x3, blocking collectives: 33.7 us -> 65 us  [the longest x2 38.9 us: tp_sum(): lax.all_to_all(x.reshape(RUN, RUN * BAND, HALF), 'tp', 0, 0, axis_index_g...]
    ppermute x2 -> x0, waiting for transfers between devices: 11 us -> none  [tp_sum(): own = own + lax.ppermute(other, 'tp', [(i, i ^ 1) for i in range(TP)])]
    ppermute x2 -> x0, starting transfers between devices: 7.57 us -> none  [tp_sum(): own = own + lax.ppermute(other, 'tp', [(i, i ^ 1) for i in range(TP)])]
    all_gather x2, blocking collectives: 56.3 us -> 49 us  [tp_sum(): return (lax.all_gather(band, 'tp'), beside)]
    unnamed x8 -> x20, local copies, waits for them, and re-layouts: 0.02 us -> 6.39 us
    all_to_all x1, waiting for transfers between devices: 7.68 us -> 2.29 us  [tp_sum(): x = lax.all_to_all(x, 'tp', 0, 0, axis_index_groups=far)]
    all_to_all x2, blocking collectives: 52.2 us -> 56.2 us  [all_sum(): terms = lax.all_to_all(x, axis, 0, 0)]
    pallas_call x13 -> x16, Pallas kernels: 33.9 us -> 30.7 us  [call(): pl.pallas_call(kernel, out_shape=out_shape, compiler_params=pltpu.Compile...]
  transfers between devices with their start and end apart: 4 -> 2, of which waited for: 4 -> 2; matrix products, arithmetic and copies ran while one was open for 0% -> 0% of each run, Pallas kernels for 4% -> 5%
where the time goes in v3:
time: 262 us; the launch traced here: 261 us
  blocking collectives  203 us (77%)
  Pallas kernels  30.7 us (12%)
  starting transfers between devices  10.7 us (4%)
  waiting for transfers between devices  9.6 us (4%)
  local copies, waits for them, and re-layouts  6.39 us (2%)
    all_to_all x2, blocking collectives, all_sum(): terms = lax.all_to_all(x, axis, 0, 0)  56.2 us
    all_gather x2, blocking collectives, tp_sum(): return (lax.all_gather(band, 'tp'), beside)  49 us
    all_to_all x2, blocking collectives, tp_sum(): lax.all_to_all(x.reshape(RUN, RUN * BAND, HALF), 'tp', 0, 0, axis_index_g...  38.9 us
    all_to_all x2, blocking collectives, all_sum(): return lax.all_to_all(call(fold_kernel, shape(*x.shape), terms), axis, 0, 0)  33 us
    pallas_call x16, Pallas kernels, call(): pl.pallas_call(kernel, out_shape=out_shape, compiler_params=pltpu.Compile...  30.7 us
    all_to_all x1, blocking collectives, tp_sum(): x = lax.all_to_all(x, 'tp', 0, 0, axis_index_groups=far)  26.1 us
    all_to_all x1, waiting for transfers between devices, local(): squares = lax.all_to_all(squares, 'tp', 0, 0)  7.31 us
    unnamed x20, local copies, waits for them, and re-layouts  6.39 us
  transfers between devices with their start and end apart: 2, of which 2 were waited for; matrix products, arithmetic and copies ran while one was open for 0% of the time, Pallas kernels for 5%

profile of v3, /device:TPU:1, one launch (start us, length us, event | category | flops | bytes accessed | tf_op | source)
XLA Modules:
  0.0 261.3 jit_solution(13420361152969127523)
XLA Ops:
  0.6 0.0 copy-start
  0.6 1.2 copy-done
  1.9 0.0 copy-start.2
  1.9 1.3 copy-done.2
  3.2 0.0 copy-start.9
  3.2 1.0 copy-done.9
  4.2 0.8 shard_map.58
  4.9 20.9 %all_to_all.45.x_ref = f32[4,288,128]{2,1,0:T(8,128)S(1)} all-to-all(f32[4,288,128]{2,1,0:T(8,128)S(1)} %bitcast.27), channel_id=1, replica_groups={{0,1,2,3},{4,5,6,7},{8,9,10,11},{12,13,14,15},{16,17,18,19},{20,21,22,2..., dimensions={0} | all-to-all | bytes 1179648 | tf_op jit(solution)/shard_map/all_to_all | solution.py:106
  25.9 26.1 %all_to_all.46.x_ref = f32[4,72,128]{2,1,0:T(8,128)S(1)} all-to-all(f32[4,72,128]{2,1,0:T(8,128)S(1)} %bitcast.28), channel_id=1, replica_groups={{0,4,8,12},{1,5,9,13},{2,6,10,14},{3,7,11,15},{16,20,24,28},{17,21,25,2..., dimensions={0} | all-to-all | bytes 294912 | tf_op jit(solution)/shard_map/all_to_all | solution.py:108
  52.0 23.4 %all-gather = f32[1152,128]{1,0:T(8,128)S(1)} all-gather(f32[72,128]{1,0:T(8,128)S(1)} %shard_map.60), channel_id=2, replica_groups=mesh['fsdp'=32,'tp'=16] {'tp'}, dimensions={0}, use_global_device_ids=true | all-gather | bytes 626688 | tf_op jit(solution)/shard_map/all_gather | solution.py:112
  75.4 1.5 shard_map.61
  76.9 29.1 %all_to_all.47.x_ref = f32[32,40,128]{2,1,0:T(8,128)S(1)} all-to-all(f32[32,40,128]{2,1,0:T(8,128)S(1)} %bitcast.20), channel_id=1, replica_groups=mesh['fsdp'=32,'tp'=16] {'fsdp'}, dimensions={0} | all-to-all | bytes 1310720 | tf_op jit(solution)/shard_map/all_to_all | solution.py:95
  106.0 0.1 shard_map.62
  106.0 16.5 %all_to_all.48 = f32[32,40,128]{2,1,0:T(8,128)S(1)} all-to-all(f32[32,40,128]{2,1,0:T(8,128)S(1)} %shard_map.62), channel_id=1, replica_groups=mesh['fsdp'=32,'tp'=16] {'fsdp'}, dimensions={0} | all-to-all | bytes 1310720 | tf_op jit(solution)/shard_map/all_to_all | solution.py:96
  122.5 0.7 shard_map.63
  123.2 18.0 %all_to_all.49.x_ref = f32[4,288,128]{2,1,0:T(8,128)S(1)} all-to-all(f32[4,288,128]{2,1,0:T(8,128)S(1)} %bitcast.25), channel_id=1, replica_groups={{0,1,2,3},{4,5,6,7},{8,9,10,11},{12,13,14,15},{16,17,18,19},{20,21,22,2..., dimensions={0} | all-to-all | bytes 1179648 | tf_op jit(solution)/shard_map/all_to_all | solution.py:106
  141.2 0.7 shard_map.64
  141.9 5.7 %all-to-all-start.5 = ((f32[4,72,128]{2,1,0:T(8,128)}), f32[4,72,128]{2,1,0:T(8,128)S(1)}, u32[]{:S(2)}, u32[]{:S(2)}) async-start(f32[4,72,128]{2,1,0:T(8,128)} %bitcast.8), calls=%async_computation.5 | async-start | bytes 294912 | tf_op jit(solution)/shard_map/all_to_all | solution.py:108
  147.6 9.8 %shard_map.66.x_ref = f32[256,256]{1,0:T(8,128)S(1)} custom-call(f32[1280,128]{1,0:T(8,128)S(1)} %bitcast.19), custom_call_target="tpu_custom_call" | custom-call | flops 20000000000 | bytes 655360 | tf_op jit(solution)/shard_map/pallas_call | solution.py:51
  157.5 2.3 all-to-all-done.5.x_ref
  159.8 25.6 %all-gather.1 = f32[1152,128]{1,0:T(8,128)S(1)} all-gather(f32[72,128]{1,0:T(8,128)S(1)} %shard_map.65), channel_id=3, replica_groups=mesh['fsdp'=32,'tp'=16] {'tp'}, dimensions={0}, use_global_device_ids=true | all-gather | bytes 626688 | tf_op jit(solution)/shard_map/all_gather | solution.py:112
  185.4 2.3 shard_map.67
  187.7 0.0 copy-start.4
  187.7 27.1 %all_to_all.50.x_ref = f32[32,40,128]{2,1,0:T(8,128)S(1)} all-to-all(f32[32,40,128]{2,1,0:T(8,128)S(1)} %bitcast.26), channel_id=1, replica_groups=mesh['fsdp'=32,'tp'=16] {'fsdp'}, dimensions={0} | all-to-all | bytes 1310720 | tf_op jit(solution)/shard_map/all_to_all | solution.py:95
  214.8 0.0 copy-done.4
  214.8 0.1 shard_map.68
  214.9 16.5 %all_to_all.51 = f32[32,40,128]{2,1,0:T(8,128)S(1)} all-to-all(f32[32,40,128]{2,1,0:T(8,128)S(1)} %shard_map.68), channel_id=1, replica_groups=mesh['fsdp'=32,'tp'=16] {'fsdp'}, dimensions={0} | all-to-all | bytes 1310720 | tf_op jit(solution)/shard_map/all_to_all | solution.py:96
  231.4 9.8 %shard_map.69.x_ref = f32[256,256]{1,0:T(8,128)S(1)} custom-call(f32[1280,128]{1,0:T(8,128)S(1)} %bitcast.21), custom_call_target="tpu_custom_call" | custom-call | flops 20000000000 | bytes 655360 | tf_op jit(solution)/shard_map/pallas_call | solution.py:51
  241.2 0.0 copy-start.1
  241.2 0.0 copy-start.3
  241.2 1.1 shard_map.71
  242.3 0.0 copy-start.6
  242.3 0.8 copy-done.6
  243.1 5.0 %all-to-all-start.8 = ((f32[16,8,128]{2,1,0:T(8,128)}), f32[16,8,128]{2,1,0:T(8,128)S(1)}, u32[]{:S(2)}, u32[]{:S(2)}) async-start(f32[16,8,128]{2,1,0:T(8,128)} %get-tuple-element.22), calls=%async_computation.8 | async-start | bytes 131072 | tf_op jit(solution)/shard_map/all_to_all | solution.py:282
  248.0 0.0 copy-start.5
  248.0 1.1 copy-done.5
  249.1 0.4 shard_map.70.q_ref
  249.5 0.0 copy-done.1
  249.6 0.0 copy-done.3
  249.6 0.0 copy-start.7
  249.6 1.0 copy-done.7
  250.6 0.0 copy-start.8
  250.6 1.7 shard_map.73
  252.3 7.3 %all-to-all-done.8.s_ref = f32[16,8,128]{2,1,0:T(8,128)S(1)} async-done(((f32[16,8,128]{2,1,0:T(8,128)}), f32[16,8,128]{2,1,0:T(8,128)S(1)}, u32[]{:S(2)}, u32[]{:S(2)}) %all-to-all-start.8) | async-done | bytes 65568 | tf_op jit(solution)/shard_map/all_to_all | solution.py:282
  259.6 0.0 copy-done.8
  259.6 1.7 shard_map.72
  (3 shorter events, 0.1 us)
Async XLA Ops:
  0.6 1.3 copy-start
  1.9 1.3 copy-start.2
  3.2 1.0 copy-start.9
  141.9 17.8 %all-to-all-start.5 = ((f32[4,72,128]{2,1,0:T(8,128)}), f32[4,72,128]{2,1,0:T(8,128)S(1)}, u32[]{:S(2)}, u32[]{:S(2)}) async-start(f32[4,72,128]{2,1,0:T(8,128)} %bitcast.8), calls=%async_computation.5 | async-start | bytes 294912 | tf_op jit(solution)/shard_map/all_to_all | solution.py:108
  187.7 27.1 %copy-start.4 = (f32[576,256]{1,0:T(8,128)}, f32[576,256]{1,0:T(8,128)S(1)}, u32[]{:S(2)}) copy-start(f32[576,256]{1,0:T(8,128)S(1)} %get-tuple-element.19.p_ref) | copy-start | bytes 1769476
  241.2 8.3 %copy-start.1 = (f32[576,448]{0,1:T(8,128)S(1)}, f32[576,448]{0,1:T(8,128)}, u32[]{:S(2)}) copy-start(f32[576,448]{0,1:T(8,128)} %param.3) | copy-start | bytes 3096580
  241.2 8.3 %copy-start.3 = (f32[576,448]{0,1:T(8,128)S(1)}, f32[576,448]{0,1:T(8,128)}, u32[]{:S(2)}) copy-start(f32[576,448]{0,1:T(8,128)} %param.4) | copy-start | bytes 3096580
  242.3 0.8 copy-start.6
  243.1 16.5 %all-to-all-start.8 = ((f32[16,8,128]{2,1,0:T(8,128)}), f32[16,8,128]{2,1,0:T(8,128)S(1)}, u32[]{:S(2)}, u32[]{:S(2)}) async-start(f32[16,8,128]{2,1,0:T(8,128)} %get-tuple-element.22), calls=%async_computation.8 | async-start | bytes 131072 | tf_op jit(solution)/shard_map/all_to_all | solution.py:282
  248.0 1.1 copy-start.5
  249.6 1.0 copy-start.7
  250.6 9.0 %copy-start.8 = (f32[448,256]{1,0:T(8,128)S(1)}, f32[448,256]{1,0:T(8,128)}, u32[]{:S(2)}) copy-start(f32[448,256]{1,0:T(8,128)} %copy-done.6) | copy-start | bytes 1376260

commit v4 on v2

--- a/solution.py
+++ b/solution.py
@@ -16,7 +16,7 @@
 ROWS = M_ROWS // FSDP
 COLS = N_COLS // TP
 BAND = 2 * ROWS // TP
-SHARE = 40
+PACKED = 2 * COLS + 3 * HALF
 
 decay_rate = 0.95
 epsilon = 1e-06
@@ -72,65 +72,44 @@
     return jnp.concatenate([x.reshape(ROWS, HALF) for x in halves], axis=1)
 
 
-def first_kernel(g_ref, m_ref, b_ref, high_ref, low_ref, own_ref, other_ref, total_ref):
-    step = pl.program_id(0)
+def first_kernel(g_ref, m_ref, b_ref, high_ref, low_ref, own_ref, other_ref):
     high, low = split(m_ref[...] + g_ref[...])
     high_ref[...] = high
     low_ref[...] = low
-    term = dot3((high, low), split(b_ref[...]), TN)
-
-    @pl.when(step == 0)
-    def _():
-        total_ref[...] = term
-
-    @pl.when(step > 0)
-    def _():
-        total_ref[...] += term
-
-    @pl.when(step == pl.num_programs(0) - 1)
-    def _():
-        put_halves(own_ref, other_ref, total_ref[...])
+    put_halves(own_ref, other_ref, dot3((high, low), split(b_ref[...]), TN))
 
 
 def first(g, m, b):
-    n = 4
     wide = shape(COLS, ROWS, dtype=BF16)
     half = shape(ROWS, HALF)
-    block = pl.BlockSpec((COLS // n, ROWS), lambda i: (i, 0))
-    whole = pl.BlockSpec((ROWS, HALF), lambda i: (0, 0))
-    return call(
-        first_kernel,
-        (wide, wide, half, half),
-        g,
-        m,
-        b,
-        flops=6 * ROWS * COLS * RANK,
-        vmem=60,
-        grid=(n,),
-        in_specs=[block, block, pl.BlockSpec((COLS // n, RANK), lambda i: (i, 0))],
-        out_specs=[block, block, whole, whole],
-        scratch_shapes=[pltpu.VMEM((ROWS, RANK), F32)],
-    )
-
-
-def fold_kernel(x_ref, out_ref):
-    out_ref[...] = jnp.broadcast_to(jnp.sum(x_ref[...], axis=0, keepdims=True), out_ref.shape)
-
-
-def all_sum(x, axis):
-    terms = lax.all_to_all(x, axis, 0, 0)
-    return lax.all_to_all(call(fold_kernel, shape(*x.shape), terms), axis, 0, 0)
-
-
-def band_kernel(x_ref, out_ref):
+    return call(first_kernel, (wide, wide, half, half), g, m, b, flops=6 * ROWS * COLS * RANK)
+
+
+def add_kernel(x_ref, out_ref):
     out_ref[...] = jnp.sum(x_ref[...], axis=0)
+
+
+def repeat_kernel(x_ref, y_ref, out_ref):
+    out_ref[...] = jnp.broadcast_to((x_ref[...] + y_ref[...])[None], out_ref.shape)
+
+
+def fsdp_sum(x):
+    chips = FSDP // 2
+    places = [list(range(core, FSDP, 2)) for core in range(2)]
+    rows = x.shape[0] // chips
+    terms = lax.all_to_all(x.reshape(chips, rows, HALF), "fsdp", 0, 0, axis_index_groups=places)
+    piece = call(add_kernel, shape(rows, HALF), terms)
+    other = lax.ppermute(piece, "fsdp", [(i, i ^ 1) for i in range(FSDP)])
+    pieces = call(repeat_kernel, shape(chips, rows, HALF), piece, other)
+    pieces = lax.all_to_all(pieces, "fsdp", 0, 0, axis_index_groups=places)
+    return pieces.reshape(chips * rows, HALF)
 
 
 def tp_sum(own, other, beside=None):
     own = own + lax.ppermute(other, "tp", [(i, i ^ 1) for i in range(TP)])
     places = [list(range(i, TP, 2)) for i in range(2)]
     terms = lax.all_to_all(own.reshape(TP // 2, BAND, HALF), "tp", 0, 0, axis_index_groups=places)
-    band = call(band_kernel, shape(BAND, HALF), terms)
+    band = call(add_kernel, shape(BAND, HALF), terms)
     if beside is not None:
         band, beside = lax.optimization_barrier((band, beside))
     return lax.all_gather(band, "tp"), beside
@@ -154,7 +133,7 @@
 
 
 def reflect(high, low, p):
-    return call(reflect_kernel, shape(FSDP * SHARE, HALF), high, low, p, flops=6 * ROWS * COLS * RANK)
+    return call(reflect_kernel, shape(PACKED, HALF), high, low, p, flops=6 * ROWS * COLS * RANK)
 
 
 def project_kernel(high_ref, low_ref, c_ref, own_ref, other_ref):
@@ -176,7 +155,7 @@
 def second_reflect(high, low, p, x):
     return call(
         second_reflect_kernel,
-        (shape(ROWS, RANK), shape(FSDP * SHARE, HALF)),
+        (shape(ROWS, RANK), shape(PACKED, HALF)),
         high,
         low,
         p,
@@ -189,16 +168,17 @@
     lanes = lambda v, k: jnp.broadcast_to(v[:, k : k + 1], (8, HALF))
     sublanes = lambda v, k: jnp.broadcast_to(v[k : k + 1, :], (8, HALF))
     n = HALF // 8
+    col_at = lax.broadcasted_iota(jnp.int32, (8, HALF), 1)
     a = [s[8 * v : 8 * v + 8, :] for v in range(n)]
-    row_at = lax.broadcasted_iota(jnp.int32, (8, HALF), 0)
-    col_at = lax.broadcasted_iota(jnp.int32, (8, HALF), 1)
-    e = [jnp.where(col_at == row_at + 8 * v, 1.0, 0.0).astype(F32) for v in range(n)]
     out = []
     for k0 in range(0, HALF, PANEL):
         place = [divmod(k0 + j, 8) for j in range(PANEL)]
+        in_panel = (col_at >= k0) & (col_at < k0 + PANEL)
         cols = {v: [lanes(a[v], k0 + j) for j in range(PANEL)] for v in range(k0 // 8, n)}
-        rows = [sublanes(a[v], k) for v, k in place]
-        units = [sublanes(e[v], k) for v, k in place]
+        rows = [
+            jnp.where(in_panel, jnp.where(col_at == k0 + j, 1.0, 0.0), sublanes(a[v], k))
+            for j, (v, k) in enumerate(place)
+        ]
         d = [[sublanes(cols[v][j], k) for j in range(i + 1)] for i, (v, k) in enumerate(place)]
         factor = [[None] * PANEL for _ in range(PANEL)]
         inverse = [None] * PANEL
@@ -222,13 +202,13 @@
                 y.append(t * inverse[j])
             return y
 
-        rows, units = solve(rows), solve(units)
-        out += [u[:1] for u in units]
+        rows = solve(rows)
+        out += [jnp.where(col_at < k0 + PANEL, row, 0.0)[:1] for row in rows]
         for v in range((k0 + PANEL) // 8, n):
+            a[v] = jnp.where(in_panel, 0.0, a[v])
             c = solve(cols[v])
             for j in range(PANEL):
                 a[v] = a[v] - c[j] * rows[j]
-                e[v] = e[v] - c[j] * units[j]
     return out
 
 
@@ -301,11 +281,11 @@
     high, low, *p = first(gradient, momentum, start_basis)
     p, _ = tp_sum(*p)
     c = reflect(high, low, p)
-    c = all_sum(c.reshape(FSDP, SHARE, HALF), "fsdp").reshape(FSDP * SHARE, HALF)
+    c = fsdp_sum(c)
     p = project(high, low, c)
     p, x = tp_sum(*p, inverse_factor(c))
     p, c = second_reflect(high, low, p, x)
-    c = all_sum(c.reshape(FSDP, SHARE, HALF), "fsdp").reshape(FSDP * SHARE, HALF)
+    c = fsdp_sum(c)
     x = inverse_factor(c)
     q, r, squares = basis(p, c, x)
     squares = lax.all_to_all(squares, "tp", 0, 0)

time: 259 us -> 255 us (0.985)
  blocking collectives: 175 us -> 146 us
  starting transfers between devices: 18.1 us -> 42.8 us
  Pallas kernels: 33.9 us -> 29 us
  local copies, waits for them, and re-layouts: 0.02 us -> 3.54 us
  waiting for transfers between devices: 28.5 us -> 31.2 us
    all_to_all x4, blocking collectives: 85.2 us -> 59.1 us  [the longest x2 30.5 us: fsdp_sum(): pieces = lax.all_to_all(pieces, 'fsdp', 0, 0, axis_index_groups=places)]
    ppermute x0 -> x2, starting transfers between devices: none -> 24.9 us  [fsdp_sum(): other = lax.ppermute(piece, 'fsdp', [(i, i ^ 1) for i in range(FSDP)])]
    pallas_call x13 -> x15, Pallas kernels: 33.9 us -> 29 us  [call(): pl.pallas_call(kernel, out_shape=out_shape, compiler_params=pltpu.Compile...]
    unnamed x8 -> x10, local copies, waits for them, and re-layouts: 0.02 us -> 3.54 us
    all_gather x2, blocking collectives: 56.3 us -> 53.2 us  [tp_sum(): return (lax.all_gather(band, 'tp'), beside)]
  transfers between devices with their start and end apart: 4 -> 6, of which waited for: 4 -> 6; matrix products, arithmetic and copies ran while one was open for 0% -> 0% of each run, Pallas kernels for 4% -> 4%
where the time goes in v4:
time: 255 us; the launch traced here: 254 us
  blocking collectives  146 us (57%)
  starting transfers between devices  42.8 us (17%)
  waiting for transfers between devices  31.2 us (12%)
  Pallas kernels  29 us (11%)
  local copies, waits for them, and re-layouts  3.54 us (1%)
    all_gather x2, blocking collectives, tp_sum(): return (lax.all_gather(band, 'tp'), beside)  53.2 us
    all_to_all x1, blocking collectives, tp_sum(): lax.all_to_all(own.reshape(TP // 2, BAND, HALF), 'tp', 0, 0, axis_index_g...  33.7 us
    all_to_all x2, blocking collectives, fsdp_sum(): pieces = lax.all_to_all(pieces, 'fsdp', 0, 0, axis_index_groups=places)  30.5 us
    pallas_call x15, Pallas kernels, call(): pl.pallas_call(kernel, out_shape=out_shape, compiler_params=pltpu.Compile...  29 us
    all_to_all x2, blocking collectives, fsdp_sum(): lax.all_to_all(x.reshape(chips, rows, HALF), 'fsdp', 0, 0, axis_index_gro...  28.7 us
    ppermute x2, starting transfers between devices, fsdp_sum(): other = lax.ppermute(piece, 'fsdp', [(i, i ^ 1) for i in range(FSDP)])  24.9 us
    all_to_all x1, waiting for transfers between devices, tp_sum(): lax.all_to_all(own.reshape(TP // 2, BAND, HALF), 'tp', 0, 0, axis_index_g...  9.98 us
    all_to_all x1, waiting for transfers between devices, local(): squares = lax.all_to_all(squares, 'tp', 0, 0)  9.84 us
  transfers between devices with their start and end apart: 6, of which 6 were waited for; matrix products, arithmetic and copies ran while one was open for 0% of the time, Pallas kernels for 4%

profile of v4, /device:TPU:1, one launch (start us, length us, event | category | flops | bytes accessed | tf_op | source)
XLA Modules:
  0.0 254.1 jit_solution(1456628142853056823)
XLA Ops:
  0.6 0.0 copy-start
  0.6 1.2 copy-done
  1.9 0.0 copy-start.2
  1.9 1.3 copy-done.2
  3.2 0.0 copy-start.4
  3.2 1.0 copy-done.4
  4.2 0.8 shard_map.58
  4.9 4.4 %collective-permute-start = (f32[576,128]{1,0:T(8,128)S(1)}, f32[576,128]{1,0:T(8,128)S(1)}, u32[]{:S(2)}, u32[]{:S(2)}) collective-permute-start(f32[576,128]{1,0:T(8,128)S(1)} %get-tuple-element.21), channel_id=1, source_target_pairs={{0,1},{1,0},{2,3},{3,2},{4,5},{5,4},{6,7},{7,6},{8,9},{9,8},{10,11... | collective-permute-start | bytes 884744 | tf_op jit(solution)/shard_map/ppermute | solution.py:109
  9.3 4.1 %collective-permute-done = f32[576,128]{1,0:T(8,128)S(1)} collective-permute-done((f32[576,128]{1,0:T(8,128)S(1)}, f32[576,128]{1,0:T(8,128)S(1)}, u32[]{:S(2)}, u32[]{:S(2)}) %collective-permute-start) | collective-permute-done | bytes 294944 | tf_op jit(solution)/shard_map/ppermute | solution.py:109
  13.5 33.7 %all_to_all.35.x_ref = f32[8,72,128]{2,1,0:T(8,128)S(1)} all-to-all(f32[8,72,128]{2,1,0:T(8,128)S(1)} %bitcast.24), channel_id=1, replica_groups={{0,2,4,6,8,10,12,14},{1,3,5,7,9,11,13,15},{16,18,20,22,24,26,28,30},{17..., dimensions={0} | all-to-all | bytes 589824 | tf_op jit(solution)/shard_map/all_to_all | solution.py:111
  47.2 28.7 %all-gather = f32[1152,128]{1,0:T(8,128)S(1)} all-gather(f32[72,128]{1,0:T(8,128)S(1)} %shard_map.59), channel_id=2, replica_groups=mesh['fsdp'=32,'tp'=16] {'tp'}, dimensions={0}, use_global_device_ids=true | all-gather | bytes 626688 | tf_op jit(solution)/shard_map/all_gather | solution.py:115
  75.8 1.5 shard_map.60
  77.3 16.2 %all_to_all.36.x_ref = f32[16,80,128]{2,1,0:T(8,128)S(1)} all-to-all(f32[16,80,128]{2,1,0:T(8,128)S(1)} %bitcast.18), channel_id=1, replica_groups={{0,32,64,96,128,160,192,224,256,288,320,352,384,416,448,480},{16,48,80,..., dimensions={0} | all-to-all | bytes 1310720 | tf_op jit(solution)/shard_map/all_to_all | solution.py:100
  93.6 11.7 %collective-permute-start.1 = (f32[80,128]{1,0:T(8,128)S(1)}, f32[80,128]{1,0:T(8,128)S(1)}, u32[]{:S(2)}, u32[]{:S(2)}) collective-permute-start(f32[80,128]{1,0:T(8,128)S(1)} %shard_map.61.x_ref), channel_id=1, source_target_pairs={{0,16},{16,0},{32,48},{48,32},{64,80},{80,64},{96,112},{112,96},{1... | collective-permute-start | bytes 122888 | tf_op jit(solution)/shard_map/ppermute | solution.py:102
  105.3 0.8 collective-permute-done.1.y_ref
  106.2 15.2 %all_to_all.37 = f32[16,80,128]{2,1,0:T(8,128)S(1)} all-to-all(f32[16,80,128]{2,1,0:T(8,128)S(1)} %shard_map.62), channel_id=1, replica_groups={{0,32,64,96,128,160,192,224,256,288,320,352,384,416,448,480},{16,48,80,..., dimensions={0} | all-to-all | bytes 1310720 | tf_op jit(solution)/shard_map/all_to_all | solution.py:104
  121.4 0.7 shard_map.63
  122.1 3.3 %collective-permute-start.2 = (f32[576,128]{1,0:T(8,128)S(1)}, f32[576,128]{1,0:T(8,128)S(1)}, u32[]{:S(2)}, u32[]{:S(2)}) collective-permute-start(f32[576,128]{1,0:T(8,128)S(1)} %get-tuple-element.23), channel_id=1, source_target_pairs={{0,1},{1,0},{2,3},{3,2},{4,5},{5,4},{6,7},{7,6},{8,9},{9,8},{10,11... | collective-permute-start | bytes 884744 | tf_op jit(solution)/shard_map/ppermute | solution.py:109
  125.4 5.6 %collective-permute-done.2 = f32[576,128]{1,0:T(8,128)S(1)} collective-permute-done((f32[576,128]{1,0:T(8,128)S(1)}, f32[576,128]{1,0:T(8,128)S(1)}, u32[]{:S(2)}, u32[]{:S(2)}) %collective-permute-start.2) | collective-permute-done | bytes 294944 | tf_op jit(solution)/shard_map/ppermute | solution.py:109
  131.0 0.7 add.7
  131.8 5.4 %all-to-all-start.3 = ((f32[8,72,128]{2,1,0:T(8,128)}), f32[8,72,128]{2,1,0:T(8,128)S(1)}, u32[]{:S(2)}, u32[]{:S(2)}) async-start(f32[8,72,128]{2,1,0:T(8,128)} %bitcast.6), calls=%async_computation.3 | async-start | bytes 589824 | tf_op jit(solution)/shard_map/all_to_all | solution.py:111
  137.2 9.4 %shard_map.65.x_ref = f32[256,256]{1,0:T(8,128)S(1)} custom-call(f32[1280,128]{1,0:T(8,128)S(1)} %bitcast.17), custom_call_target="tpu_custom_call" | custom-call | flops 20000000000 | bytes 655360 | tf_op jit(solution)/shard_map/pallas_call | solution.py:50
  146.6 10.0 %all-to-all-done.3.x_ref = f32[8,72,128]{2,1,0:T(8,128)S(1)} async-done(((f32[8,72,128]{2,1,0:T(8,128)}), f32[8,72,128]{2,1,0:T(8,128)S(1)}, u32[]{:S(2)}, u32[]{:S(2)}) %all-to-all-start.3) | async-done | bytes 294944 | tf_op jit(solution)/shard_map/all_to_all | solution.py:111
  156.6 24.5 %all-gather.1 = f32[1152,128]{1,0:T(8,128)S(1)} all-gather(f32[72,128]{1,0:T(8,128)S(1)} %shard_map.64), channel_id=3, replica_groups=mesh['fsdp'=32,'tp'=16] {'tp'}, dimensions={0}, use_global_device_ids=true | all-gather | bytes 626688 | tf_op jit(solution)/shard_map/all_gather | solution.py:115
  181.1 2.3 shard_map.66
  183.4 12.4 %all_to_all.38.x_ref = f32[16,80,128]{2,1,0:T(8,128)S(1)} all-to-all(f32[16,80,128]{2,1,0:T(8,128)S(1)} %bitcast.23), channel_id=1, replica_groups={{0,32,64,96,128,160,192,224,256,288,320,352,384,416,448,480},{16,48,80,..., dimensions={0} | all-to-all | bytes 1310720 | tf_op jit(solution)/shard_map/all_to_all | solution.py:100
  195.8 13.2 %collective-permute-start.3 = (f32[80,128]{1,0:T(8,128)S(1)}, f32[80,128]{1,0:T(8,128)S(1)}, u32[]{:S(2)}, u32[]{:S(2)}) collective-permute-start(f32[80,128]{1,0:T(8,128)S(1)} %shard_map.67.x_ref), channel_id=1, source_target_pairs={{0,16},{16,0},{32,48},{48,32},{64,80},{80,64},{96,112},{112,96},{1... | collective-permute-start | bytes 122888 | tf_op jit(solution)/shard_map/ppermute | solution.py:102
  209.1 0.8 collective-permute-done.3.y_ref
  210.0 15.2 %all_to_all.39 = f32[16,80,128]{2,1,0:T(8,128)S(1)} all-to-all(f32[16,80,128]{2,1,0:T(8,128)S(1)} %shard_map.68), channel_id=1, replica_groups={{0,32,64,96,128,160,192,224,256,288,320,352,384,416,448,480},{16,48,80,..., dimensions={0} | all-to-all | bytes 1310720 | tf_op jit(solution)/shard_map/all_to_all | solution.py:104
  225.2 0.0 copy-start.3
  225.2 9.4 %shard_map.69.x_ref = f32[256,256]{1,0:T(8,128)S(1)} custom-call(f32[1280,128]{1,0:T(8,128)S(1)} %bitcast.19), custom_call_target="tpu_custom_call" | custom-call | flops 20000000000 | bytes 655360 | tf_op jit(solution)/shard_map/pallas_call | solution.py:50
  234.6 0.0 copy-start.1
  234.6 1.3 shard_map.70
  235.9 4.8 %all-to-all-start.6 = ((f32[16,8,128]{2,1,0:T(8,128)}), f32[16,8,128]{2,1,0:T(8,128)S(1)}, u32[]{:S(2)}, u32[]{:S(2)}) async-start(f32[16,8,128]{2,1,0:T(8,128)} %get-tuple-element.30), calls=%async_computation.6 | async-start | bytes 131072 | tf_op jit(solution)/shard_map/all_to_all | solution.py:291
  240.8 0.0 copy-done.3
  240.8 0.0 copy-done.1
  240.8 1.7 shard_map.72
  242.5 9.8 %all-to-all-done.6.s_ref = f32[16,8,128]{2,1,0:T(8,128)S(1)} async-done(((f32[16,8,128]{2,1,0:T(8,128)}), f32[16,8,128]{2,1,0:T(8,128)S(1)}, u32[]{:S(2)}, u32[]{:S(2)}) %all-to-all-start.6) | async-done | bytes 65568 | tf_op jit(solution)/shard_map/all_to_all | solution.py:291
  252.4 1.7 shard_map.71
  (7 shorter events, 0.2 us)
Async XLA Ops:
  0.6 1.3 copy-start
  1.9 1.3 copy-start.2
  3.2 1.0 copy-start.4
  4.9 8.5 %collective-permute-start = (f32[576,128]{1,0:T(8,128)S(1)}, f32[576,128]{1,0:T(8,128)S(1)}, u32[]{:S(2)}, u32[]{:S(2)}) collective-permute-start(f32[576,128]{1,0:T(8,128)S(1)} %get-tuple-element.21), channel_id=1, source_target_pairs={{0,1},{1,0},{2,3},{3,2},{4,5},{5,4},{6,7},{7,6},{8,9},{9,8},{10,11... | collective-permute-start | bytes 884744 | tf_op jit(solution)/shard_map/ppermute | solution.py:109
  93.6 12.5 %collective-permute-start.1 = (f32[80,128]{1,0:T(8,128)S(1)}, f32[80,128]{1,0:T(8,128)S(1)}, u32[]{:S(2)}, u32[]{:S(2)}) collective-permute-start(f32[80,128]{1,0:T(8,128)S(1)} %shard_map.61.x_ref), channel_id=1, source_target_pairs={{0,16},{16,0},{32,48},{48,32},{64,80},{80,64},{96,112},{112,96},{1... | collective-permute-start | bytes 122888 | tf_op jit(solution)/shard_map/ppermute | solution.py:102
  122.1 8.9 %collective-permute-start.2 = (f32[576,128]{1,0:T(8,128)S(1)}, f32[576,128]{1,0:T(8,128)S(1)}, u32[]{:S(2)}, u32[]{:S(2)}) collective-permute-start(f32[576,128]{1,0:T(8,128)S(1)} %get-tuple-element.23), channel_id=1, source_target_pairs={{0,1},{1,0},{2,3},{3,2},{4,5},{5,4},{6,7},{7,6},{8,9},{9,8},{10,11... | collective-permute-start | bytes 884744 | tf_op jit(solution)/shard_map/ppermute | solution.py:109
  131.8 24.8 %all-to-all-start.3 = ((f32[8,72,128]{2,1,0:T(8,128)}), f32[8,72,128]{2,1,0:T(8,128)S(1)}, u32[]{:S(2)}, u32[]{:S(2)}) async-start(f32[8,72,128]{2,1,0:T(8,128)} %bitcast.6), calls=%async_computation.3 | async-start | bytes 589824 | tf_op jit(solution)/shard_map/all_to_all | solution.py:111
  195.8 14.1 %collective-permute-start.3 = (f32[80,128]{1,0:T(8,128)S(1)}, f32[80,128]{1,0:T(8,128)S(1)}, u32[]{:S(2)}, u32[]{:S(2)}) collective-permute-start(f32[80,128]{1,0:T(8,128)S(1)} %shard_map.67.x_ref), channel_id=1, source_target_pairs={{0,16},{16,0},{32,48},{48,32},{64,80},{80,64},{96,112},{112,96},{1... | collective-permute-start | bytes 122888 | tf_op jit(solution)/shard_map/ppermute | solution.py:102
  225.2 15.6 %copy-start.3 = (f32[576,448]{0,1:T(8,128)S(1)}, f32[576,448]{0,1:T(8,128)}, u32[]{:S(2)}) copy-start(f32[576,448]{0,1:T(8,128)} %param.4) | copy-start | bytes 3096580
  234.6 6.2 %copy-start.1 = (f32[576,448]{0,1:T(8,128)S(1)}, f32[576,448]{0,1:T(8,128)}, u32[]{:S(2)}) copy-start(f32[576,448]{0,1:T(8,128)} %param.3) | copy-start | bytes 3096580
  235.9 16.4 %all-to-all-start.6 = ((f32[16,8,128]{2,1,0:T(8,128)}), f32[16,8,128]{2,1,0:T(8,128)S(1)}, u32[]{:S(2)}, u32[]{:S(2)}) async-start(f32[16,8,128]{2,1,0:T(8,128)} %get-tuple-element.30), calls=%async_computation.6 | async-start | bytes 131072 | tf_op jit(solution)/shard_map/all_to_all | solution.py:291

commit v5 on v4

--- a/solution.py
+++ b/solution.py
@@ -72,17 +72,17 @@
     return jnp.concatenate([x.reshape(ROWS, HALF) for x in halves], axis=1)
 
 
-def first_kernel(g_ref, m_ref, b_ref, high_ref, low_ref, own_ref, other_ref):
-    high, low = split(m_ref[...] + g_ref[...])
+def first_kernel(a_ref, b_ref, high_ref, low_ref, own_ref, other_ref):
+    high, low = split(a_ref[...])
     high_ref[...] = high
     low_ref[...] = low
     put_halves(own_ref, other_ref, dot3((high, low), split(b_ref[...]), TN))
 
 
-def first(g, m, b):
+def first(a, b):
     wide = shape(COLS, ROWS, dtype=BF16)
     half = shape(ROWS, HALF)
-    return call(first_kernel, (wide, wide, half, half), g, m, b, flops=6 * ROWS * COLS * RANK)
+    return call(first_kernel, (wide, wide, half, half), a, b, flops=6 * ROWS * COLS * RANK)
 
 
 def add_kernel(x_ref, out_ref):
@@ -262,9 +262,9 @@
     )
 
 
-def momentum_kernel(g_ref, m_ref, q_ref, r_ref, out_ref):
+def momentum_kernel(a_ref, q_ref, r_ref, out_ref):
     product = dot3(split(r_ref[...]), split(q_ref[...]), NT)
-    out_ref[...] = (m_ref[...] + g_ref[...]) - (1.0 - decay_rate) * product
+    out_ref[...] = a_ref[...] - (1.0 - decay_rate) * product
 
 
 def update_kernel(q_ref, r_ref, s_ref, out_ref, d_ref):
@@ -277,8 +277,8 @@
 
 
 def local(gradient, momentum, start_basis):
-    gradient, momentum = gradient.T, momentum.T
-    high, low, *p = first(gradient, momentum, start_basis)
+    combined = momentum.T + gradient.T
+    high, low, *p = first(combined, start_basis)
     p, _ = tp_sum(*p)
     c = reflect(high, low, p)
     c = fsdp_sum(c)
@@ -290,7 +290,7 @@
     q, r, squares = basis(p, c, x)
     squares = lax.all_to_all(squares, "tp", 0, 0)
     flops = 6 * ROWS * COLS * RANK
-    new_momentum = call(momentum_kernel, shape(COLS, ROWS), gradient, momentum, q, r, flops=flops)
+    new_momentum = call(momentum_kernel, shape(COLS, ROWS), combined, q, r, flops=flops)
     update, directions = call(
         update_kernel, (shape(COLS, ROWS), shape(COLS, RANK)), q, r, squares, flops=flops
     )

time: 255 us -> 253 us (level)
  local copies, waits for them, and re-layouts: 3.54 us -> 0.01 us
    unnamed x10 -> x2, local copies, waits for them, and re-layouts: 3.54 us -> 0.01 us
where the time goes in v5:
time: 253 us; the launch traced here: 252 us
  blocking collectives  146 us (58%)
  starting transfers between devices  42.8 us (17%)
  waiting for transfers between devices  31.3 us (12%)
  Pallas kernels  28.9 us (11%)
  other arithmetic  2.55 us (1%)
    all_gather x2, blocking collectives, tp_sum(): return (lax.all_gather(band, 'tp'), beside)  53.2 us
    all_to_all x1, blocking collectives, tp_sum(): lax.all_to_all(own.reshape(TP // 2, BAND, HALF), 'tp', 0, 0, axis_index_g...  33.7 us
    all_to_all x2, blocking collectives, fsdp_sum(): pieces = lax.all_to_all(pieces, 'fsdp', 0, 0, axis_index_groups=places)  30.5 us
    pallas_call x15, Pallas kernels, call(): pl.pallas_call(kernel, out_shape=out_shape, compiler_params=pltpu.Compile...  28.9 us
    all_to_all x2, blocking collectives, fsdp_sum(): lax.all_to_all(x.reshape(chips, rows, HALF), 'fsdp', 0, 0, axis_index_gro...  28.6 us
    ppermute x2, starting transfers between devices, fsdp_sum(): other = lax.ppermute(piece, 'fsdp', [(i, i ^ 1) for i in range(FSDP)])  24.9 us
    all_to_all x1, waiting for transfers between devices, tp_sum(): lax.all_to_all(own.reshape(TP // 2, BAND, HALF), 'tp', 0, 0, axis_index_g...  9.97 us
    all_to_all x1, waiting for transfers between devices, local(): squares = lax.all_to_all(squares, 'tp', 0, 0)  9.86 us
  transfers between devices with their start and end apart: 6, of which 6 were waited for; matrix products, arithmetic and copies ran while one was open for 0% of the time, Pallas kernels for 4%

profile of v5, /device:TPU:1, one launch (start us, length us, event | category | flops | bytes accessed | tf_op | source)
XLA Modules:
  0.0 252.3 jit_solution(15774987346324425426)
XLA Ops:
  0.6 0.0 copy-start
  0.6 1.8 add_bitcast_fusion.a_ref
  2.4 0.0 copy-done
  2.4 0.7 shard_map.58
  3.2 4.4 %collective-permute-start = (f32[576,128]{1,0:T(8,128)S(1)}, f32[576,128]{1,0:T(8,128)S(1)}, u32[]{:S(2)}, u32[]{:S(2)}) collective-permute-start(f32[576,128]{1,0:T(8,128)S(1)} %get-tuple-element.21), channel_id=1, source_target_pairs={{0,1},{1,0},{2,3},{3,2},{4,5},{5,4},{6,7},{7,6},{8,9},{9,8},{10,11... | collective-permute-start | bytes 884744 | tf_op jit(solution)/shard_map/ppermute | solution.py:109
  7.6 4.1 %collective-permute-done = f32[576,128]{1,0:T(8,128)S(1)} collective-permute-done((f32[576,128]{1,0:T(8,128)S(1)}, f32[576,128]{1,0:T(8,128)S(1)}, u32[]{:S(2)}, u32[]{:S(2)}) %collective-permute-start) | collective-permute-done | bytes 294944 | tf_op jit(solution)/shard_map/ppermute | solution.py:109
  11.7 33.7 %all_to_all.35.x_ref = f32[8,72,128]{2,1,0:T(8,128)S(1)} all-to-all(f32[8,72,128]{2,1,0:T(8,128)S(1)} %bitcast.20), channel_id=1, replica_groups={{0,2,4,6,8,10,12,14},{1,3,5,7,9,11,13,15},{16,18,20,22,24,26,28,30},{17..., dimensions={0} | all-to-all | bytes 589824 | tf_op jit(solution)/shard_map/all_to_all | solution.py:111
  45.4 28.7 %all-gather = f32[1152,128]{1,0:T(8,128)S(1)} all-gather(f32[72,128]{1,0:T(8,128)S(1)} %shard_map.59), channel_id=2, replica_groups=mesh['fsdp'=32,'tp'=16] {'tp'}, dimensions={0}, use_global_device_ids=true | all-gather | bytes 626688 | tf_op jit(solution)/shard_map/all_gather | solution.py:115
  74.1 1.5 shard_map.60
  75.6 16.2 %all_to_all.36.x_ref = f32[16,80,128]{2,1,0:T(8,128)S(1)} all-to-all(f32[16,80,128]{2,1,0:T(8,128)S(1)} %bitcast.14), channel_id=1, replica_groups={{0,32,64,96,128,160,192,224,256,288,320,352,384,416,448,480},{16,48,80,..., dimensions={0} | all-to-all | bytes 1310720 | tf_op jit(solution)/shard_map/all_to_all | solution.py:100
  91.8 11.7 %collective-permute-start.1 = (f32[80,128]{1,0:T(8,128)S(1)}, f32[80,128]{1,0:T(8,128)S(1)}, u32[]{:S(2)}, u32[]{:S(2)}) collective-permute-start(f32[80,128]{1,0:T(8,128)S(1)} %shard_map.61.x_ref), channel_id=1, source_target_pairs={{0,16},{16,0},{32,48},{48,32},{64,80},{80,64},{96,112},{112,96},{1... | collective-permute-start | bytes 122888 | tf_op jit(solution)/shard_map/ppermute | solution.py:102
  103.5 0.8 collective-permute-done.1.y_ref
  104.4 15.2 %all_to_all.37 = f32[16,80,128]{2,1,0:T(8,128)S(1)} all-to-all(f32[16,80,128]{2,1,0:T(8,128)S(1)} %shard_map.62), channel_id=1, replica_groups={{0,32,64,96,128,160,192,224,256,288,320,352,384,416,448,480},{16,48,80,..., dimensions={0} | all-to-all | bytes 1310720 | tf_op jit(solution)/shard_map/all_to_all | solution.py:104
  119.7 0.7 shard_map.63
  120.4 3.2 %collective-permute-start.2 = (f32[576,128]{1,0:T(8,128)S(1)}, f32[576,128]{1,0:T(8,128)S(1)}, u32[]{:S(2)}, u32[]{:S(2)}) collective-permute-start(f32[576,128]{1,0:T(8,128)S(1)} %get-tuple-element.23), channel_id=1, source_target_pairs={{0,1},{1,0},{2,3},{3,2},{4,5},{5,4},{6,7},{7,6},{8,9},{9,8},{10,11... | collective-permute-start | bytes 884744 | tf_op jit(solution)/shard_map/ppermute | solution.py:109
  123.6 5.7 %collective-permute-done.2 = f32[576,128]{1,0:T(8,128)S(1)} collective-permute-done((f32[576,128]{1,0:T(8,128)S(1)}, f32[576,128]{1,0:T(8,128)S(1)}, u32[]{:S(2)}, u32[]{:S(2)}) %collective-permute-start.2) | collective-permute-done | bytes 294944 | tf_op jit(solution)/shard_map/ppermute | solution.py:109
  129.3 0.7 add.14
  130.1 5.5 %all-to-all-start.3 = ((f32[8,72,128]{2,1,0:T(8,128)}), f32[8,72,128]{2,1,0:T(8,128)S(1)}, u32[]{:S(2)}, u32[]{:S(2)}) async-start(f32[8,72,128]{2,1,0:T(8,128)} %bitcast.5), calls=%async_computation.3 | async-start | bytes 589824 | tf_op jit(solution)/shard_map/all_to_all | solution.py:111
  135.5 9.4 %shard_map.65.x_ref = f32[256,256]{1,0:T(8,128)S(1)} custom-call(f32[1280,128]{1,0:T(8,128)S(1)} %bitcast.13), custom_call_target="tpu_custom_call" | custom-call | flops 20000000000 | bytes 655360 | tf_op jit(solution)/shard_map/pallas_call | solution.py:50
  144.9 10.0 %all-to-all-done.3.x_ref = f32[8,72,128]{2,1,0:T(8,128)S(1)} async-done(((f32[8,72,128]{2,1,0:T(8,128)}), f32[8,72,128]{2,1,0:T(8,128)S(1)}, u32[]{:S(2)}, u32[]{:S(2)}) %all-to-all-start.3) | async-done | bytes 294944 | tf_op jit(solution)/shard_map/all_to_all | solution.py:111
  154.9 24.5 %all-gather.1 = f32[1152,128]{1,0:T(8,128)S(1)} all-gather(f32[72,128]{1,0:T(8,128)S(1)} %shard_map.64), channel_id=3, replica_groups=mesh['fsdp'=32,'tp'=16] {'tp'}, dimensions={0}, use_global_device_ids=true | all-gather | bytes 626688 | tf_op jit(solution)/shard_map/all_gather | solution.py:115
  179.4 2.3 shard_map.66
  181.7 12.4 %all_to_all.38.x_ref = f32[16,80,128]{2,1,0:T(8,128)S(1)} all-to-all(f32[16,80,128]{2,1,0:T(8,128)S(1)} %bitcast.19), channel_id=1, replica_groups={{0,32,64,96,128,160,192,224,256,288,320,352,384,416,448,480},{16,48,80,..., dimensions={0} | all-to-all | bytes 1310720 | tf_op jit(solution)/shard_map/all_to_all | solution.py:100
  194.1 13.2 %collective-permute-start.3 = (f32[80,128]{1,0:T(8,128)S(1)}, f32[80,128]{1,0:T(8,128)S(1)}, u32[]{:S(2)}, u32[]{:S(2)}) collective-permute-start(f32[80,128]{1,0:T(8,128)S(1)} %shard_map.67.x_ref), channel_id=1, source_target_pairs={{0,16},{16,0},{32,48},{48,32},{64,80},{80,64},{96,112},{112,96},{1... | collective-permute-start | bytes 122888 | tf_op jit(solution)/shard_map/ppermute | solution.py:102
  207.4 0.8 collective-permute-done.3.y_ref
  208.3 15.2 %all_to_all.39 = f32[16,80,128]{2,1,0:T(8,128)S(1)} all-to-all(f32[16,80,128]{2,1,0:T(8,128)S(1)} %shard_map.68), channel_id=1, replica_groups={{0,32,64,96,128,160,192,224,256,288,320,352,384,416,448,480},{16,48,80,..., dimensions={0} | all-to-all | bytes 1310720 | tf_op jit(solution)/shard_map/all_to_all | solution.py:104
  223.5 9.4 %shard_map.69.x_ref = f32[256,256]{1,0:T(8,128)S(1)} custom-call(f32[1280,128]{1,0:T(8,128)S(1)} %bitcast.15), custom_call_target="tpu_custom_call" | custom-call | flops 20000000000 | bytes 655360 | tf_op jit(solution)/shard_map/pallas_call | solution.py:50
  232.9 1.3 shard_map.70
  234.2 4.7 %all-to-all-start.6 = ((f32[16,8,128]{2,1,0:T(8,128)}), f32[16,8,128]{2,1,0:T(8,128)S(1)}, u32[]{:S(2)}, u32[]{:S(2)}) async-start(f32[16,8,128]{2,1,0:T(8,128)} %get-tuple-element.30), calls=%async_computation.6 | async-start | bytes 131072 | tf_op jit(solution)/shard_map/all_to_all | solution.py:291
  239.0 1.7 shard_map.72
  240.7 9.9 %all-to-all-done.6.s_ref = f32[16,8,128]{2,1,0:T(8,128)S(1)} async-done(((f32[16,8,128]{2,1,0:T(8,128)}), f32[16,8,128]{2,1,0:T(8,128)S(1)}, u32[]{:S(2)}, u32[]{:S(2)}) %all-to-all-start.6) | async-done | bytes 65568 | tf_op jit(solution)/shard_map/all_to_all | solution.py:291
  250.6 1.7 shard_map.71
  (7 shorter events, 0.2 us)
Async XLA Ops:
  0.6 1.8 copy-start
  3.2 8.5 %collective-permute-start = (f32[576,128]{1,0:T(8,128)S(1)}, f32[576,128]{1,0:T(8,128)S(1)}, u32[]{:S(2)}, u32[]{:S(2)}) collective-permute-start(f32[576,128]{1,0:T(8,128)S(1)} %get-tuple-element.21), channel_id=1, source_target_pairs={{0,1},{1,0},{2,3},{3,2},{4,5},{5,4},{6,7},{7,6},{8,9},{9,8},{10,11... | collective-permute-start | bytes 884744 | tf_op jit(solution)/shard_map/ppermute | solution.py:109
  91.8 12.6 %collective-permute-start.1 = (f32[80,128]{1,0:T(8,128)S(1)}, f32[80,128]{1,0:T(8,128)S(1)}, u32[]{:S(2)}, u32[]{:S(2)}) collective-permute-start(f32[80,128]{1,0:T(8,128)S(1)} %shard_map.61.x_ref), channel_id=1, source_target_pairs={{0,16},{16,0},{32,48},{48,32},{64,80},{80,64},{96,112},{112,96},{1... | collective-permute-start | bytes 122888 | tf_op jit(solution)/shard_map/ppermute | solution.py:102
  120.4 8.9 %collective-permute-start.2 = (f32[576,128]{1,0:T(8,128)S(1)}, f32[576,128]{1,0:T(8,128)S(1)}, u32[]{:S(2)}, u32[]{:S(2)}) collective-permute-start(f32[576,128]{1,0:T(8,128)S(1)} %get-tuple-element.23), channel_id=1, source_target_pairs={{0,1},{1,0},{2,3},{3,2},{4,5},{5,4},{6,7},{7,6},{8,9},{9,8},{10,11... | collective-permute-start | bytes 884744 | tf_op jit(solution)/shard_map/ppermute | solution.py:109
  130.1 24.8 %all-to-all-start.3 = ((f32[8,72,128]{2,1,0:T(8,128)}), f32[8,72,128]{2,1,0:T(8,128)S(1)}, u32[]{:S(2)}, u32[]{:S(2)}) async-start(f32[8,72,128]{2,1,0:T(8,128)} %bitcast.5), calls=%async_computation.3 | async-start | bytes 589824 | tf_op jit(solution)/shard_map/all_to_all | solution.py:111
  194.1 14.1 %collective-permute-start.3 = (f32[80,128]{1,0:T(8,128)S(1)}, f32[80,128]{1,0:T(8,128)S(1)}, u32[]{:S(2)}, u32[]{:S(2)}) collective-permute-start(f32[80,128]{1,0:T(8,128)S(1)} %shard_map.67.x_ref), channel_id=1, source_target_pairs={{0,16},{16,0},{32,48},{48,32},{64,80},{80,64},{96,112},{112,96},{1... | collective-permute-start | bytes 122888 | tf_op jit(solution)/shard_map/ppermute | solution.py:102
  234.2 16.3 %all-to-all-start.6 = ((f32[16,8,128]{2,1,0:T(8,128)}), f32[16,8,128]{2,1,0:T(8,128)S(1)}, u32[]{:S(2)}, u32[]{:S(2)}) async-start(f32[16,8,128]{2,1,0:T(8,128)} %get-tuple-element.30), calls=%async_computation.6 | async-start | bytes 131072 | tf_op jit(solution)/shard_map/all_to_all | solution.py:291

commit v6 on v5

--- a/solution.py
+++ b/solution.py
@@ -118,9 +118,9 @@
 def put_reflected(ref, c, p):
     for h in range(2):
         ref[h * COLS : (h + 1) * COLS, :] = c[:, h * HALF : (h + 1) * HALF]
-    left, right = p[:, :HALF], p[:, HALF:]
-    for i, (a, b) in enumerate(((left, left), (right, left), (right, right))):
-        ref[2 * COLS + i * HALF : 2 * COLS + (i + 1) * HALF, :] = dot6(a, b, TN)
+    gram = dot6(p, p, TN)
+    for i, (a, b) in enumerate(((0, 0), (HALF, 0), (HALF, HALF))):
+        ref[2 * COLS + i * HALF : 2 * COLS + (i + 1) * HALF, :] = gram[a : a + HALF, b : b + HALF]
 
 
 def get_reflected(ref):
@@ -240,40 +240,39 @@
     )
 
 
-def basis_kernel(p_ref, c_ref, x_ref, q_ref, r_ref, s_ref):
-    x = split(x_ref[...])
-    q_ref[...] = dot3(split(p_ref[...]), x, NT)
-    r = dot3(split(get_reflected(c_ref)), x, NT)
-    r_ref[...] = r
+def squares_kernel(c_ref, x_ref, s_ref):
+    r = dot3(split(get_reflected(c_ref)), split(x_ref[...]), NT)
     squares = jnp.sum(r * r, axis=0, keepdims=True)
     for h in range(2):
         half = squares[:, h * HALF : (h + 1) * HALF]
         s_ref[:, 4 * h : 4 * h + 4, :] = jnp.broadcast_to(half[None], (TP, 4, HALF))
 
 
+def basis_kernel(p_ref, c_ref, x_ref, high_ref, low_ref, r_ref):
+    x = split(x_ref[...])
+    high_ref[...], low_ref[...] = split(dot3(split(p_ref[...]), x, NT))
+    r_ref[...] = dot3(split(get_reflected(c_ref)), x, NT)
+
+
 def basis(p, c, x):
-    return call(
-        basis_kernel,
-        (shape(ROWS, RANK), shape(COLS, RANK), shape(TP, 8, HALF)),
-        p,
-        c,
-        x,
-        flops=6 * (ROWS + COLS) * RANK * RANK,
-    )
-
-
-def momentum_kernel(a_ref, q_ref, r_ref, out_ref):
-    product = dot3(split(r_ref[...]), split(q_ref[...]), NT)
+    half = shape(ROWS, RANK, dtype=BF16)
+    flops = 6 * (ROWS + COLS) * RANK * RANK
+    return call(basis_kernel, (half, half, shape(COLS, RANK)), p, c, x, flops=flops)
+
+
+def momentum_kernel(a_ref, high_ref, low_ref, r_ref, out_ref):
+    product = dot3(split(r_ref[...]), (high_ref[...], low_ref[...]), NT)
     out_ref[...] = a_ref[...] - (1.0 - decay_rate) * product
 
 
-def update_kernel(q_ref, r_ref, s_ref, out_ref, d_ref):
+def update_kernel(high_ref, low_ref, r_ref, s_ref, out_ref, d_ref):
     squares = jnp.sum(s_ref[...], axis=0)
     scale = lax.rsqrt(squares / N_COLS + epsilon)
     scale = jnp.concatenate([scale[:1], scale[4:5]], axis=1)
     d = r_ref[...] * scale
     d_ref[...] = d
-    out_ref[...] = math.sqrt(M_ROWS / RANK) * dot3(split(d), split(q_ref[...]), NT)
+    product = dot3(split(d), (high_ref[...], low_ref[...]), NT)
+    out_ref[...] = math.sqrt(M_ROWS / RANK) * product
 
 
 def local(gradient, momentum, start_basis):
@@ -287,12 +286,13 @@
     p, c = second_reflect(high, low, p, x)
     c = fsdp_sum(c)
     x = inverse_factor(c)
-    q, r, squares = basis(p, c, x)
+    squares = call(squares_kernel, shape(TP, 8, HALF), c, x, flops=6 * COLS * RANK * RANK)
     squares = lax.all_to_all(squares, "tp", 0, 0)
+    *q, r = basis(p, c, x)
     flops = 6 * ROWS * COLS * RANK
-    new_momentum = call(momentum_kernel, shape(COLS, ROWS), combined, q, r, flops=flops)
+    new_momentum = call(momentum_kernel, shape(COLS, ROWS), combined, *q, r, flops=flops)
     update, directions = call(
-        update_kernel, (shape(COLS, ROWS), shape(COLS, RANK)), q, r, squares, flops=flops
+        update_kernel, (shape(COLS, ROWS), shape(COLS, RANK)), *q, r, squares, flops=flops
     )
     return (update.T, new_momentum.T, directions)
 

time: 253 us -> 255 us (level)
  local copies, waits for them, and re-layouts: 0.01 us -> 3.35 us
    unnamed x2 -> x10, local copies, waits for them, and re-layouts: 0.01 us -> 3.35 us
    pallas_call x15 -> x16, Pallas kernels: 28.9 us -> 28.8 us  [call(): pl.pallas_call(kernel, out_shape=out_shape, compiler_params=pltpu.Compile...]
  transfers between devices with their start and end apart: 6 -> 6, of which waited for: 6 -> 6; matrix products, arithmetic and copies ran while one was open for 0% -> 0% of each run, Pallas kernels for 4% -> 5%
where the time goes in v6:
time: 255 us; the launch traced here: 254 us
  blocking collectives  146 us (57%)
  starting transfers between devices  42.8 us (17%)
  waiting for transfers between devices  29.3 us (11%)
  Pallas kernels  28.8 us (11%)
  local copies, waits for them, and re-layouts  3.35 us (1%)
    all_gather x2, blocking collectives, tp_sum(): return (lax.all_gather(band, 'tp'), beside)  53.4 us
    all_to_all x1, blocking collectives, tp_sum(): lax.all_to_all(own.reshape(TP // 2, BAND, HALF), 'tp', 0, 0, axis_index_g...  33.7 us
    all_to_all x2, blocking collectives, fsdp_sum(): pieces = lax.all_to_all(pieces, 'fsdp', 0, 0, axis_index_groups=places)  30.5 us
    pallas_call x16, Pallas kernels, call(): pl.pallas_call(kernel, out_shape=out_shape, compiler_params=pltpu.Compile...  28.8 us
    all_to_all x2, blocking collectives, fsdp_sum(): lax.all_to_all(x.reshape(chips, rows, HALF), 'fsdp', 0, 0, axis_index_gro...  28.6 us
    ppermute x2, starting transfers between devices, fsdp_sum(): other = lax.ppermute(piece, 'fsdp', [(i, i ^ 1) for i in range(FSDP)])  25 us
    all_to_all x1, waiting for transfers between devices, tp_sum(): lax.all_to_all(own.reshape(TP // 2, BAND, HALF), 'tp', 0, 0, axis_index_g...  9.97 us
    ppermute x2, waiting for transfers between devices, tp_sum(): own = own + lax.ppermute(other, 'tp', [(i, i ^ 1) for i in range(TP)])  9.79 us
  transfers between devices with their start and end apart: 6, of which 6 were waited for; matrix products, arithmetic and copies ran while one was open for 0% of the time, Pallas kernels for 5%

profile of v6, /device:TPU:1, one launch (start us, length us, event | category | flops | bytes accessed | tf_op | source)
XLA Modules:
  0.0 253.6 jit_solution(1236705746342677279)
XLA Ops:
  0.6 0.0 copy-start
  0.6 1.8 add_bitcast_fusion.a_ref
  2.4 0.0 copy-done
  2.4 0.7 shard_map.58
  3.2 4.4 %collective-permute-start = (f32[576,128]{1,0:T(8,128)S(1)}, f32[576,128]{1,0:T(8,128)S(1)}, u32[]{:S(2)}, u32[]{:S(2)}) collective-permute-start(f32[576,128]{1,0:T(8,128)S(1)} %get-tuple-element.21), channel_id=1, source_target_pairs={{0,1},{1,0},{2,3},{3,2},{4,5},{5,4},{6,7},{7,6},{8,9},{9,8},{10,11... | collective-permute-start | bytes 884744 | tf_op jit(solution)/shard_map/ppermute | solution.py:109
  7.6 4.1 %collective-permute-done = f32[576,128]{1,0:T(8,128)S(1)} collective-permute-done((f32[576,128]{1,0:T(8,128)S(1)}, f32[576,128]{1,0:T(8,128)S(1)}, u32[]{:S(2)}, u32[]{:S(2)}) %collective-permute-start) | collective-permute-done | bytes 294944 | tf_op jit(solution)/shard_map/ppermute | solution.py:109
  11.7 33.7 %all_to_all.35.x_ref = f32[8,72,128]{2,1,0:T(8,128)S(1)} all-to-all(f32[8,72,128]{2,1,0:T(8,128)S(1)} %bitcast.21), channel_id=1, replica_groups={{0,2,4,6,8,10,12,14},{1,3,5,7,9,11,13,15},{16,18,20,22,24,26,28,30},{17..., dimensions={0} | all-to-all | bytes 589824 | tf_op jit(solution)/shard_map/all_to_all | solution.py:111
  45.4 28.7 %all-gather = f32[1152,128]{1,0:T(8,128)S(1)} all-gather(f32[72,128]{1,0:T(8,128)S(1)} %shard_map.59), channel_id=2, replica_groups=mesh['fsdp'=32,'tp'=16] {'tp'}, dimensions={0}, use_global_device_ids=true | all-gather | bytes 626688 | tf_op jit(solution)/shard_map/all_gather | solution.py:115
  74.1 1.4 shard_map.60
  75.5 16.2 %all_to_all.36.x_ref = f32[16,80,128]{2,1,0:T(8,128)S(1)} all-to-all(f32[16,80,128]{2,1,0:T(8,128)S(1)} %bitcast.17), channel_id=1, replica_groups={{0,32,64,96,128,160,192,224,256,288,320,352,384,416,448,480},{16,48,80,..., dimensions={0} | all-to-all | bytes 1310720 | tf_op jit(solution)/shard_map/all_to_all | solution.py:100
  91.7 11.7 %collective-permute-start.1 = (f32[80,128]{1,0:T(8,128)S(1)}, f32[80,128]{1,0:T(8,128)S(1)}, u32[]{:S(2)}, u32[]{:S(2)}) collective-permute-start(f32[80,128]{1,0:T(8,128)S(1)} %shard_map.61.x_ref), channel_id=1, source_target_pairs={{0,16},{16,0},{32,48},{48,32},{64,80},{80,64},{96,112},{112,96},{1... | collective-permute-start | bytes 122888 | tf_op jit(solution)/shard_map/ppermute | solution.py:102
  103.4 0.8 collective-permute-done.1.y_ref
  104.3 15.2 %all_to_all.37 = f32[16,80,128]{2,1,0:T(8,128)S(1)} all-to-all(f32[16,80,128]{2,1,0:T(8,128)S(1)} %shard_map.62), channel_id=1, replica_groups={{0,32,64,96,128,160,192,224,256,288,320,352,384,416,448,480},{16,48,80,..., dimensions={0} | all-to-all | bytes 1310720 | tf_op jit(solution)/shard_map/all_to_all | solution.py:104
  119.6 0.7 shard_map.63
  120.3 3.2 %collective-permute-start.2 = (f32[576,128]{1,0:T(8,128)S(1)}, f32[576,128]{1,0:T(8,128)S(1)}, u32[]{:S(2)}, u32[]{:S(2)}) collective-permute-start(f32[576,128]{1,0:T(8,128)S(1)} %get-tuple-element.23), channel_id=1, source_target_pairs={{0,1},{1,0},{2,3},{3,2},{4,5},{5,4},{6,7},{7,6},{8,9},{9,8},{10,11... | collective-permute-start | bytes 884744 | tf_op jit(solution)/shard_map/ppermute | solution.py:109
  123.5 5.7 %collective-permute-done.2 = f32[576,128]{1,0:T(8,128)S(1)} collective-permute-done((f32[576,128]{1,0:T(8,128)S(1)}, f32[576,128]{1,0:T(8,128)S(1)}, u32[]{:S(2)}, u32[]{:S(2)}) %collective-permute-start.2) | collective-permute-done | bytes 294944 | tf_op jit(solution)/shard_map/ppermute | solution.py:109
  129.2 0.7 add.14
  129.9 5.5 %all-to-all-start.3 = ((f32[8,72,128]{2,1,0:T(8,128)}), f32[8,72,128]{2,1,0:T(8,128)S(1)}, u32[]{:S(2)}, u32[]{:S(2)}) async-start(f32[8,72,128]{2,1,0:T(8,128)} %bitcast.5), calls=%async_computation.3 | async-start | bytes 589824 | tf_op jit(solution)/shard_map/all_to_all | solution.py:111
  135.4 9.4 %shard_map.65.x_ref = f32[256,256]{1,0:T(8,128)S(1)} custom-call(f32[1280,128]{1,0:T(8,128)S(1)} %bitcast.16), custom_call_target="tpu_custom_call" | custom-call | flops 20000000000 | bytes 655360 | tf_op jit(solution)/shard_map/pallas_call | solution.py:50
  144.8 10.0 %all-to-all-done.3.x_ref = f32[8,72,128]{2,1,0:T(8,128)S(1)} async-done(((f32[8,72,128]{2,1,0:T(8,128)}), f32[8,72,128]{2,1,0:T(8,128)S(1)}, u32[]{:S(2)}, u32[]{:S(2)}) %all-to-all-start.3) | async-done | bytes 294944 | tf_op jit(solution)/shard_map/all_to_all | solution.py:111
  154.8 24.7 %all-gather.1 = f32[1152,128]{1,0:T(8,128)S(1)} all-gather(f32[72,128]{1,0:T(8,128)S(1)} %shard_map.64), channel_id=3, replica_groups=mesh['fsdp'=32,'tp'=16] {'tp'}, dimensions={0}, use_global_device_ids=true | all-gather | bytes 626688 | tf_op jit(solution)/shard_map/all_gather | solution.py:115
  179.5 1.8 shard_map.66
  181.4 12.4 %all_to_all.38.x_ref = f32[16,80,128]{2,1,0:T(8,128)S(1)} all-to-all(f32[16,80,128]{2,1,0:T(8,128)S(1)} %bitcast.20), channel_id=1, replica_groups={{0,32,64,96,128,160,192,224,256,288,320,352,384,416,448,480},{16,48,80,..., dimensions={0} | all-to-all | bytes 1310720 | tf_op jit(solution)/shard_map/all_to_all | solution.py:100
  193.8 13.2 %collective-permute-start.3 = (f32[80,128]{1,0:T(8,128)S(1)}, f32[80,128]{1,0:T(8,128)S(1)}, u32[]{:S(2)}, u32[]{:S(2)}) collective-permute-start(f32[80,128]{1,0:T(8,128)S(1)} %shard_map.67.x_ref), channel_id=1, source_target_pairs={{0,16},{16,0},{32,48},{48,32},{64,80},{80,64},{96,112},{112,96},{1... | collective-permute-start | bytes 122888 | tf_op jit(solution)/shard_map/ppermute | solution.py:102
  207.0 0.8 collective-permute-done.3.y_ref
  207.9 15.2 %all_to_all.39 = f32[16,80,128]{2,1,0:T(8,128)S(1)} all-to-all(f32[16,80,128]{2,1,0:T(8,128)S(1)} %shard_map.68), channel_id=1, replica_groups={{0,32,64,96,128,160,192,224,256,288,320,352,384,416,448,480},{16,48,80,..., dimensions={0} | all-to-all | bytes 1310720 | tf_op jit(solution)/shard_map/all_to_all | solution.py:104
  223.2 9.4 %shard_map.69.x_ref = f32[256,256]{1,0:T(8,128)S(1)} custom-call(f32[1280,128]{1,0:T(8,128)S(1)} %bitcast.12), custom_call_target="tpu_custom_call" | custom-call | flops 20000000000 | bytes 655360 | tf_op jit(solution)/shard_map/pallas_call | solution.py:50
  232.6 1.1 shard_map.71
  233.7 4.7 %all-to-all-start.6 = ((f32[16,8,128]{2,1,0:T(8,128)}), f32[16,8,128]{2,1,0:T(8,128)S(1)}, u32[]{:S(2)}, u32[]{:S(2)}) async-start(f32[16,8,128]{2,1,0:T(8,128)} %shard_map.71), calls=%async_computation.6 | async-start | bytes 131072 | tf_op jit(solution)/shard_map/all_to_all | solution.py:290
  238.4 0.6 shard_map.70
  239.0 1.7 shard_map.73
  240.7 0.0 copy-start.1
  240.7 0.7 copy-done.1
  241.4 0.0 copy-start.3
  241.4 0.7 copy-done.3
  242.2 7.8 %all-to-all-done.6.s_ref = f32[16,8,128]{2,1,0:T(8,128)S(1)} async-done(((f32[16,8,128]{2,1,0:T(8,128)}), f32[16,8,128]{2,1,0:T(8,128)S(1)}, u32[]{:S(2)}, u32[]{:S(2)}) %all-to-all-start.6) | async-done | bytes 65568 | tf_op jit(solution)/shard_map/all_to_all | solution.py:290
  250.0 0.0 copy-start.2
  250.0 1.0 copy-done.2
  250.9 0.0 copy-start.4
  250.9 1.0 copy-done.4
  251.9 1.7 shard_map.72
  (7 shorter events, 0.2 us)
Async XLA Ops:
  0.6 1.8 copy-start
  3.2 8.5 %collective-permute-start = (f32[576,128]{1,0:T(8,128)S(1)}, f32[576,128]{1,0:T(8,128)S(1)}, u32[]{:S(2)}, u32[]{:S(2)}) collective-permute-start(f32[576,128]{1,0:T(8,128)S(1)} %get-tuple-element.21), channel_id=1, source_target_pairs={{0,1},{1,0},{2,3},{3,2},{4,5},{5,4},{6,7},{7,6},{8,9},{9,8},{10,11... | collective-permute-start | bytes 884744 | tf_op jit(solution)/shard_map/ppermute | solution.py:109
  91.7 12.6 %collective-permute-start.1 = (f32[80,128]{1,0:T(8,128)S(1)}, f32[80,128]{1,0:T(8,128)S(1)}, u32[]{:S(2)}, u32[]{:S(2)}) collective-permute-start(f32[80,128]{1,0:T(8,128)S(1)} %shard_map.61.x_ref), channel_id=1, source_target_pairs={{0,16},{16,0},{32,48},{48,32},{64,80},{80,64},{96,112},{112,96},{1... | collective-permute-start | bytes 122888 | tf_op jit(solution)/shard_map/ppermute | solution.py:102
  120.3 8.9 %collective-permute-start.2 = (f32[576,128]{1,0:T(8,128)S(1)}, f32[576,128]{1,0:T(8,128)S(1)}, u32[]{:S(2)}, u32[]{:S(2)}) collective-permute-start(f32[576,128]{1,0:T(8,128)S(1)} %get-tuple-element.23), channel_id=1, source_target_pairs={{0,1},{1,0},{2,3},{3,2},{4,5},{5,4},{6,7},{7,6},{8,9},{9,8},{10,11... | collective-permute-start | bytes 884744 | tf_op jit(solution)/shard_map/ppermute | solution.py:109
  129.9 24.9 %all-to-all-start.3 = ((f32[8,72,128]{2,1,0:T(8,128)}), f32[8,72,128]{2,1,0:T(8,128)S(1)}, u32[]{:S(2)}, u32[]{:S(2)}) async-start(f32[8,72,128]{2,1,0:T(8,128)} %bitcast.5), calls=%async_computation.3 | async-start | bytes 589824 | tf_op jit(solution)/shard_map/all_to_all | solution.py:111
  193.8 14.1 %collective-permute-start.3 = (f32[80,128]{1,0:T(8,128)S(1)}, f32[80,128]{1,0:T(8,128)S(1)}, u32[]{:S(2)}, u32[]{:S(2)}) collective-permute-start(f32[80,128]{1,0:T(8,128)S(1)} %shard_map.67.x_ref), channel_id=1, source_target_pairs={{0,16},{16,0},{32,48},{48,32},{64,80},{80,64},{96,112},{112,96},{1... | collective-permute-start | bytes 122888 | tf_op jit(solution)/shard_map/ppermute | solution.py:102
  233.7 16.3 %all-to-all-start.6 = ((f32[16,8,128]{2,1,0:T(8,128)}), f32[16,8,128]{2,1,0:T(8,128)S(1)}, u32[]{:S(2)}, u32[]{:S(2)}) async-start(f32[16,8,128]{2,1,0:T(8,128)} %shard_map.71), calls=%async_computation.6 | async-start | bytes 131072 | tf_op jit(solution)/shard_map/all_to_all | solution.py:290
  240.7 0.7 copy-start.1
  241.4 0.7 copy-start.3
  250.0 1.0 copy-start.2
  250.9 1.0 copy-start.4

commit v7 on v5

--- a/solution.py
+++ b/solution.py
@@ -118,9 +118,9 @@
 def put_reflected(ref, c, p):
     for h in range(2):
         ref[h * COLS : (h + 1) * COLS, :] = c[:, h * HALF : (h + 1) * HALF]
-    left, right = p[:, :HALF], p[:, HALF:]
-    for i, (a, b) in enumerate(((left, left), (right, left), (right, right))):
-        ref[2 * COLS + i * HALF : 2 * COLS + (i + 1) * HALF, :] = dot6(a, b, TN)
+    gram = dot6(p, p, TN)
+    for i, (a, b) in enumerate(((0, 0), (HALF, 0), (HALF, HALF))):
+        ref[2 * COLS + i * HALF : 2 * COLS + (i + 1) * HALF, :] = gram[a : a + HALF, b : b + HALF]
 
 
 def get_reflected(ref):

time: 253 us -> 253 us (level)
  no operation moved by 1% of the time
where the time goes in v7:
time: 253 us; the launch traced here: 252 us
  blocking collectives  146 us (58%)
  starting transfers between devices  42.8 us (17%)
  waiting for transfers between devices  31.3 us (12%)
  Pallas kernels  28.4 us (11%)
  other arithmetic  2.55 us (1%)
    all_gather x2, blocking collectives, tp_sum(): return (lax.all_gather(band, 'tp'), beside)  53.4 us
    all_to_all x1, blocking collectives, tp_sum(): lax.all_to_all(own.reshape(TP // 2, BAND, HALF), 'tp', 0, 0, axis_index_g...  33.7 us
    all_to_all x2, blocking collectives, fsdp_sum(): pieces = lax.all_to_all(pieces, 'fsdp', 0, 0, axis_index_groups=places)  30.5 us
    all_to_all x2, blocking collectives, fsdp_sum(): lax.all_to_all(x.reshape(chips, rows, HALF), 'fsdp', 0, 0, axis_index_gro...  28.6 us
    pallas_call x15, Pallas kernels, call(): pl.pallas_call(kernel, out_shape=out_shape, compiler_params=pltpu.Compile...  28.4 us
    ppermute x2, starting transfers between devices, fsdp_sum(): other = lax.ppermute(piece, 'fsdp', [(i, i ^ 1) for i in range(FSDP)])  25 us
    all_to_all x1, waiting for transfers between devices, tp_sum(): lax.all_to_all(own.reshape(TP // 2, BAND, HALF), 'tp', 0, 0, axis_index_g...  9.97 us
    all_to_all x1, waiting for transfers between devices, local(): squares = lax.all_to_all(squares, 'tp', 0, 0)  9.86 us
  transfers between devices with their start and end apart: 6, of which 6 were waited for; matrix products, arithmetic and copies ran while one was open for 0% of the time, Pallas kernels for 4%

profile of v7, /device:TPU:1, one launch (start us, length us, event | category | flops | bytes accessed | tf_op | source)
XLA Modules:
  0.0 252.0 jit_solution(16082121955522767968)
XLA Ops:
  0.6 0.0 copy-start
  0.6 1.8 add_bitcast_fusion.a_ref
  2.4 0.0 copy-done
  2.4 0.7 shard_map.58
  3.2 4.4 %collective-permute-start = (f32[576,128]{1,0:T(8,128)S(1)}, f32[576,128]{1,0:T(8,128)S(1)}, u32[]{:S(2)}, u32[]{:S(2)}) collective-permute-start(f32[576,128]{1,0:T(8,128)S(1)} %get-tuple-element.21), channel_id=1, source_target_pairs={{0,1},{1,0},{2,3},{3,2},{4,5},{5,4},{6,7},{7,6},{8,9},{9,8},{10,11... | collective-permute-start | bytes 884744 | tf_op jit(solution)/shard_map/ppermute | solution.py:109
  7.6 4.1 %collective-permute-done = f32[576,128]{1,0:T(8,128)S(1)} collective-permute-done((f32[576,128]{1,0:T(8,128)S(1)}, f32[576,128]{1,0:T(8,128)S(1)}, u32[]{:S(2)}, u32[]{:S(2)}) %collective-permute-start) | collective-permute-done | bytes 294944 | tf_op jit(solution)/shard_map/ppermute | solution.py:109
  11.7 33.7 %all_to_all.35.x_ref = f32[8,72,128]{2,1,0:T(8,128)S(1)} all-to-all(f32[8,72,128]{2,1,0:T(8,128)S(1)} %bitcast.20), channel_id=1, replica_groups={{0,2,4,6,8,10,12,14},{1,3,5,7,9,11,13,15},{16,18,20,22,24,26,28,30},{17..., dimensions={0} | all-to-all | bytes 589824 | tf_op jit(solution)/shard_map/all_to_all | solution.py:111
  45.4 28.7 %all-gather = f32[1152,128]{1,0:T(8,128)S(1)} all-gather(f32[72,128]{1,0:T(8,128)S(1)} %shard_map.59), channel_id=2, replica_groups=mesh['fsdp'=32,'tp'=16] {'tp'}, dimensions={0}, use_global_device_ids=true | all-gather | bytes 626688 | tf_op jit(solution)/shard_map/all_gather | solution.py:115
  74.1 1.4 shard_map.60
  75.5 16.2 %all_to_all.36.x_ref = f32[16,80,128]{2,1,0:T(8,128)S(1)} all-to-all(f32[16,80,128]{2,1,0:T(8,128)S(1)} %bitcast.14), channel_id=1, replica_groups={{0,32,64,96,128,160,192,224,256,288,320,352,384,416,448,480},{16,48,80,..., dimensions={0} | all-to-all | bytes 1310720 | tf_op jit(solution)/shard_map/all_to_all | solution.py:100
  91.7 11.7 %collective-permute-start.1 = (f32[80,128]{1,0:T(8,128)S(1)}, f32[80,128]{1,0:T(8,128)S(1)}, u32[]{:S(2)}, u32[]{:S(2)}) collective-permute-start(f32[80,128]{1,0:T(8,128)S(1)} %shard_map.61.x_ref), channel_id=1, source_target_pairs={{0,16},{16,0},{32,48},{48,32},{64,80},{80,64},{96,112},{112,96},{1... | collective-permute-start | bytes 122888 | tf_op jit(solution)/shard_map/ppermute | solution.py:102
  103.4 0.8 collective-permute-done.1.y_ref
  104.3 15.2 %all_to_all.37 = f32[16,80,128]{2,1,0:T(8,128)S(1)} all-to-all(f32[16,80,128]{2,1,0:T(8,128)S(1)} %shard_map.62), channel_id=1, replica_groups={{0,32,64,96,128,160,192,224,256,288,320,352,384,416,448,480},{16,48,80,..., dimensions={0} | all-to-all | bytes 1310720 | tf_op jit(solution)/shard_map/all_to_all | solution.py:104
  119.6 0.7 shard_map.63
  120.3 3.2 %collective-permute-start.2 = (f32[576,128]{1,0:T(8,128)S(1)}, f32[576,128]{1,0:T(8,128)S(1)}, u32[]{:S(2)}, u32[]{:S(2)}) collective-permute-start(f32[576,128]{1,0:T(8,128)S(1)} %get-tuple-element.23), channel_id=1, source_target_pairs={{0,1},{1,0},{2,3},{3,2},{4,5},{5,4},{6,7},{7,6},{8,9},{9,8},{10,11... | collective-permute-start | bytes 884744 | tf_op jit(solution)/shard_map/ppermute | solution.py:109
  123.5 5.7 %collective-permute-done.2 = f32[576,128]{1,0:T(8,128)S(1)} collective-permute-done((f32[576,128]{1,0:T(8,128)S(1)}, f32[576,128]{1,0:T(8,128)S(1)}, u32[]{:S(2)}, u32[]{:S(2)}) %collective-permute-start.2) | collective-permute-done | bytes 294944 | tf_op jit(solution)/shard_map/ppermute | solution.py:109
  129.2 0.7 add.14
  129.9 5.5 %all-to-all-start.3 = ((f32[8,72,128]{2,1,0:T(8,128)}), f32[8,72,128]{2,1,0:T(8,128)S(1)}, u32[]{:S(2)}, u32[]{:S(2)}) async-start(f32[8,72,128]{2,1,0:T(8,128)} %bitcast.5), calls=%async_computation.3 | async-start | bytes 589824 | tf_op jit(solution)/shard_map/all_to_all | solution.py:111
  135.4 9.4 %shard_map.65.x_ref = f32[256,256]{1,0:T(8,128)S(1)} custom-call(f32[1280,128]{1,0:T(8,128)S(1)} %bitcast.13), custom_call_target="tpu_custom_call" | custom-call | flops 20000000000 | bytes 655360 | tf_op jit(solution)/shard_map/pallas_call | solution.py:50
  144.8 10.0 %all-to-all-done.3.x_ref = f32[8,72,128]{2,1,0:T(8,128)S(1)} async-done(((f32[8,72,128]{2,1,0:T(8,128)}), f32[8,72,128]{2,1,0:T(8,128)S(1)}, u32[]{:S(2)}, u32[]{:S(2)}) %all-to-all-start.3) | async-done | bytes 294944 | tf_op jit(solution)/shard_map/all_to_all | solution.py:111
  154.8 24.7 %all-gather.1 = f32[1152,128]{1,0:T(8,128)S(1)} all-gather(f32[72,128]{1,0:T(8,128)S(1)} %shard_map.64), channel_id=3, replica_groups=mesh['fsdp'=32,'tp'=16] {'tp'}, dimensions={0}, use_global_device_ids=true | all-gather | bytes 626688 | tf_op jit(solution)/shard_map/all_gather | solution.py:115
  179.5 1.8 shard_map.66
  181.4 12.4 %all_to_all.38.x_ref = f32[16,80,128]{2,1,0:T(8,128)S(1)} all-to-all(f32[16,80,128]{2,1,0:T(8,128)S(1)} %bitcast.19), channel_id=1, replica_groups={{0,32,64,96,128,160,192,224,256,288,320,352,384,416,448,480},{16,48,80,..., dimensions={0} | all-to-all | bytes 1310720 | tf_op jit(solution)/shard_map/all_to_all | solution.py:100
  193.8 13.2 %collective-permute-start.3 = (f32[80,128]{1,0:T(8,128)S(1)}, f32[80,128]{1,0:T(8,128)S(1)}, u32[]{:S(2)}, u32[]{:S(2)}) collective-permute-start(f32[80,128]{1,0:T(8,128)S(1)} %shard_map.67.x_ref), channel_id=1, source_target_pairs={{0,16},{16,0},{32,48},{48,32},{64,80},{80,64},{96,112},{112,96},{1... | collective-permute-start | bytes 122888 | tf_op jit(solution)/shard_map/ppermute | solution.py:102
  207.0 0.8 collective-permute-done.3.y_ref
  207.9 15.2 %all_to_all.39 = f32[16,80,128]{2,1,0:T(8,128)S(1)} all-to-all(f32[16,80,128]{2,1,0:T(8,128)S(1)} %shard_map.68), channel_id=1, replica_groups={{0,32,64,96,128,160,192,224,256,288,320,352,384,416,448,480},{16,48,80,..., dimensions={0} | all-to-all | bytes 1310720 | tf_op jit(solution)/shard_map/all_to_all | solution.py:104
  223.2 9.4 %shard_map.69.x_ref = f32[256,256]{1,0:T(8,128)S(1)} custom-call(f32[1280,128]{1,0:T(8,128)S(1)} %bitcast.15), custom_call_target="tpu_custom_call" | custom-call | flops 20000000000 | bytes 655360 | tf_op jit(solution)/shard_map/pallas_call | solution.py:50
  232.6 1.3 shard_map.70
  233.9 4.7 %all-to-all-start.6 = ((f32[16,8,128]{2,1,0:T(8,128)}), f32[16,8,128]{2,1,0:T(8,128)S(1)}, u32[]{:S(2)}, u32[]{:S(2)}) async-start(f32[16,8,128]{2,1,0:T(8,128)} %get-tuple-element.30), calls=%async_computation.6 | async-start | bytes 131072 | tf_op jit(solution)/shard_map/all_to_all | solution.py:291
  238.6 1.7 shard_map.72
  240.4 9.9 %all-to-all-done.6.s_ref = f32[16,8,128]{2,1,0:T(8,128)S(1)} async-done(((f32[16,8,128]{2,1,0:T(8,128)}), f32[16,8,128]{2,1,0:T(8,128)S(1)}, u32[]{:S(2)}, u32[]{:S(2)}) %all-to-all-start.6) | async-done | bytes 65568 | tf_op jit(solution)/shard_map/all_to_all | solution.py:291
  250.2 1.7 shard_map.71
  (7 shorter events, 0.2 us)
Async XLA Ops:
  0.6 1.8 copy-start
  3.2 8.5 %collective-permute-start = (f32[576,128]{1,0:T(8,128)S(1)}, f32[576,128]{1,0:T(8,128)S(1)}, u32[]{:S(2)}, u32[]{:S(2)}) collective-permute-start(f32[576,128]{1,0:T(8,128)S(1)} %get-tuple-element.21), channel_id=1, source_target_pairs={{0,1},{1,0},{2,3},{3,2},{4,5},{5,4},{6,7},{7,6},{8,9},{9,8},{10,11... | collective-permute-start | bytes 884744 | tf_op jit(solution)/shard_map/ppermute | solution.py:109
  91.7 12.6 %collective-permute-start.1 = (f32[80,128]{1,0:T(8,128)S(1)}, f32[80,128]{1,0:T(8,128)S(1)}, u32[]{:S(2)}, u32[]{:S(2)}) collective-permute-start(f32[80,128]{1,0:T(8,128)S(1)} %shard_map.61.x_ref), channel_id=1, source_target_pairs={{0,16},{16,0},{32,48},{48,32},{64,80},{80,64},{96,112},{112,96},{1... | collective-permute-start | bytes 122888 | tf_op jit(solution)/shard_map/ppermute | solution.py:102
  120.3 8.9 %collective-permute-start.2 = (f32[576,128]{1,0:T(8,128)S(1)}, f32[576,128]{1,0:T(8,128)S(1)}, u32[]{:S(2)}, u32[]{:S(2)}) collective-permute-start(f32[576,128]{1,0:T(8,128)S(1)} %get-tuple-element.23), channel_id=1, source_target_pairs={{0,1},{1,0},{2,3},{3,2},{4,5},{5,4},{6,7},{7,6},{8,9},{9,8},{10,11... | collective-permute-start | bytes 884744 | tf_op jit(solution)/shard_map/ppermute | solution.py:109
  129.9 24.9 %all-to-all-start.3 = ((f32[8,72,128]{2,1,0:T(8,128)}), f32[8,72,128]{2,1,0:T(8,128)S(1)}, u32[]{:S(2)}, u32[]{:S(2)}) async-start(f32[8,72,128]{2,1,0:T(8,128)} %bitcast.5), calls=%async_computation.3 | async-start | bytes 589824 | tf_op jit(solution)/shard_map/all_to_all | solution.py:111
  193.8 14.1 %collective-permute-start.3 = (f32[80,128]{1,0:T(8,128)S(1)}, f32[80,128]{1,0:T(8,128)S(1)}, u32[]{:S(2)}, u32[]{:S(2)}) collective-permute-start(f32[80,128]{1,0:T(8,128)S(1)} %shard_map.67.x_ref), channel_id=1, source_target_pairs={{0,16},{16,0},{32,48},{48,32},{64,80},{80,64},{96,112},{112,96},{1... | collective-permute-start | bytes 122888 | tf_op jit(solution)/shard_map/ppermute | solution.py:102
  233.9 16.3 %all-to-all-start.6 = ((f32[16,8,128]{2,1,0:T(8,128)}), f32[16,8,128]{2,1,0:T(8,128)S(1)}, u32[]{:S(2)}, u32[]{:S(2)}) async-start(f32[16,8,128]{2,1,0:T(8,128)} %get-tuple-element.30), calls=%async_computation.6 | async-start | bytes 131072 | tf_op jit(solution)/shard_map/all_to_all | solution.py:291

commit v8 on v7

--- a/solution.py
+++ b/solution.py
@@ -1,3 +1,4 @@
+import functools
 import math
 
 import jax
@@ -60,11 +61,10 @@
     return jax.ShapeDtypeStruct(dims, dtype)
 
 
-def put_halves(own_ref, other_ref, value):
-    left, right = value[:, :HALF], value[:, HALF:]
+def half_of(x, own):
     even = lax.rem(lax.axis_index("tp"), 2) == 0
-    own_ref[...] = jnp.where(even, left, right)
-    other_ref[...] = jnp.where(even, right, left)
+    left, right = x[:, :HALF], x[:, HALF:]
+    return jnp.where(even, left, right) if own else jnp.where(even, right, left)
 
 
 def get_bands(ref):
@@ -72,17 +72,21 @@
     return jnp.concatenate([x.reshape(ROWS, HALF) for x in halves], axis=1)
 
 
-def first_kernel(a_ref, b_ref, high_ref, low_ref, own_ref, other_ref):
+def first_kernel(a_ref, b_ref, high_ref, low_ref, other_ref):
     high, low = split(a_ref[...])
     high_ref[...] = high
     low_ref[...] = low
-    put_halves(own_ref, other_ref, dot3((high, low), split(b_ref[...]), TN))
+    other_ref[...] = dot3((high, low), split(half_of(b_ref[...], False)), TN)
 
 
 def first(a, b):
     wide = shape(COLS, ROWS, dtype=BF16)
     half = shape(ROWS, HALF)
-    return call(first_kernel, (wide, wide, half, half), a, b, flops=6 * ROWS * COLS * RANK)
+    return call(first_kernel, (wide, wide, half), a, b, flops=3 * ROWS * COLS * RANK)
+
+
+def first_own_kernel(high_ref, low_ref, b_ref, own_ref):
+    own_ref[...] = dot3((high_ref[...], low_ref[...]), split(half_of(b_ref[...], True)), TN)
 
 
 def add_kernel(x_ref, out_ref):
@@ -136,14 +140,14 @@
     return call(reflect_kernel, shape(PACKED, HALF), high, low, p, flops=6 * ROWS * COLS * RANK)
 
 
-def project_kernel(high_ref, low_ref, c_ref, own_ref, other_ref):
-    c = split(get_reflected(c_ref))
-    put_halves(own_ref, other_ref, dot3((high_ref[...], low_ref[...]), c, TN))
-
-
-def project(high, low, c):
-    half = shape(ROWS, HALF)
-    return call(project_kernel, (half, half), high, low, c, flops=6 * ROWS * COLS * RANK)
+def project_kernel(own, high_ref, low_ref, c_ref, out_ref):
+    c = split(half_of(get_reflected(c_ref), own))
+    out_ref[...] = dot3((high_ref[...], low_ref[...]), c, TN)
+
+
+def project(high, low, c, own):
+    kernel = functools.partial(project_kernel, own)
+    return call(kernel, shape(ROWS, HALF), high, low, c, flops=3 * ROWS * COLS * RANK)
 
 
 def second_reflect_kernel(high_ref, low_ref, p_ref, x_ref, p_out_ref, out_ref):
@@ -278,12 +282,14 @@
 
 def local(gradient, momentum, start_basis):
     combined = momentum.T + gradient.T
-    high, low, *p = first(combined, start_basis)
-    p, _ = tp_sum(*p)
+    high, low, other = first(combined, start_basis)
+    flops = 3 * ROWS * COLS * RANK
+    own = call(first_own_kernel, shape(ROWS, HALF), high, low, start_basis, flops=flops)
+    p, _ = tp_sum(own, other)
     c = reflect(high, low, p)
     c = fsdp_sum(c)
-    p = project(high, low, c)
-    p, x = tp_sum(*p, inverse_factor(c))
+    other, own = project(high, low, c, False), project(high, low, c, True)
+    p, x = tp_sum(own, other, inverse_factor(c))
     p, c = second_reflect(high, low, p, x)
     c = fsdp_sum(c)
     x = inverse_factor(c)

time: 253 us -> 253 us (level)
    pallas_call x15 -> x17, Pallas kernels: 28.4 us -> 29.8 us  [call(): pl.pallas_call(kernel, out_shape=out_shape, compiler_params=pltpu.Compile...]
  transfers between devices with their start and end apart: 6 -> 6, of which waited for: 6 -> 6; matrix products, arithmetic and copies ran while one was open for 0% -> 0% of each run, Pallas kernels for 4% -> 5%
where the time goes in v8:
time: 253 us; the launch traced here: 252 us
  blocking collectives  146 us (58%)
  starting transfers between devices  42.8 us (17%)
  waiting for transfers between devices  30 us (12%)
  Pallas kernels  29.8 us (12%)
  other arithmetic  2.55 us (1%)
    all_gather x2, blocking collectives, tp_sum(): return (lax.all_gather(band, 'tp'), beside)  53.2 us
    all_to_all x1, blocking collectives, tp_sum(): lax.all_to_all(own.reshape(TP // 2, BAND, HALF), 'tp', 0, 0, axis_index_g...  33.7 us
    all_to_all x2, blocking collectives, fsdp_sum(): pieces = lax.all_to_all(pieces, 'fsdp', 0, 0, axis_index_groups=places)  30.5 us
    pallas_call x17, Pallas kernels, call(): pl.pallas_call(kernel, out_shape=out_shape, compiler_params=pltpu.Compile...  29.8 us
    all_to_all x2, blocking collectives, fsdp_sum(): lax.all_to_all(x.reshape(chips, rows, HALF), 'fsdp', 0, 0, axis_index_gro...  28.7 us
    ppermute x2, starting transfers between devices, fsdp_sum(): other = lax.ppermute(piece, 'fsdp', [(i, i ^ 1) for i in range(FSDP)])  24.9 us
    all_to_all x1, waiting for transfers between devices, tp_sum(): lax.all_to_all(own.reshape(TP // 2, BAND, HALF), 'tp', 0, 0, axis_index_g...  9.98 us
    all_to_all x1, waiting for transfers between devices, local(): squares = lax.all_to_all(squares, 'tp', 0, 0)  9.86 us
  transfers between devices with their start and end apart: 6, of which 6 were waited for; matrix products, arithmetic and copies ran while one was open for 0% of the time, Pallas kernels for 5%

profile of v8, /device:TPU:1, one launch (start us, length us, event | category | flops | bytes accessed | tf_op | source)
XLA Modules:
  0.0 251.8 jit_solution(11783452273588413374)
XLA Ops:
  0.6 0.0 copy-start
  0.6 1.8 add_bitcast_fusion.a_ref
  2.4 0.0 copy-done
  2.4 0.7 shard_map.58
  3.1 4.4 %collective-permute-start = (f32[576,128]{1,0:T(8,128)S(1)}, f32[576,128]{1,0:T(8,128)S(1)}, u32[]{:S(2)}, u32[]{:S(2)}) collective-permute-start(f32[576,128]{1,0:T(8,128)S(1)} %get-tuple-element.17), channel_id=1, source_target_pairs={{0,1},{1,0},{2,3},{3,2},{4,5},{5,4},{6,7},{7,6},{8,9},{9,8},{10,11... | collective-permute-start | bytes 884744 | tf_op jit(solution)/shard_map/ppermute | solution.py:113
  7.5 0.7 shard_map.59
  8.2 3.4 %collective-permute-done = f32[576,128]{1,0:T(8,128)S(1)} collective-permute-done((f32[576,128]{1,0:T(8,128)S(1)}, f32[576,128]{1,0:T(8,128)S(1)}, u32[]{:S(2)}, u32[]{:S(2)}) %collective-permute-start) | collective-permute-done | bytes 294944 | tf_op jit(solution)/shard_map/ppermute | solution.py:113
  11.7 33.7 %all_to_all.35.x_ref = f32[8,72,128]{2,1,0:T(8,128)S(1)} all-to-all(f32[8,72,128]{2,1,0:T(8,128)S(1)} %bitcast.21), channel_id=1, replica_groups={{0,2,4,6,8,10,12,14},{1,3,5,7,9,11,13,15},{16,18,20,22,24,26,28,30},{17..., dimensions={0} | all-to-all | bytes 589824 | tf_op jit(solution)/shard_map/all_to_all | solution.py:115
  45.4 28.7 %all-gather = f32[1152,128]{1,0:T(8,128)S(1)} all-gather(f32[72,128]{1,0:T(8,128)S(1)} %shard_map.60), channel_id=2, replica_groups=mesh['fsdp'=32,'tp'=16] {'tp'}, dimensions={0}, use_global_device_ids=true | all-gather | bytes 626688 | tf_op jit(solution)/shard_map/all_gather | solution.py:119
  74.0 1.4 shard_map.61
  75.4 16.3 %all_to_all.36.x_ref = f32[16,80,128]{2,1,0:T(8,128)S(1)} all-to-all(f32[16,80,128]{2,1,0:T(8,128)S(1)} %bitcast.15), channel_id=1, replica_groups={{0,32,64,96,128,160,192,224,256,288,320,352,384,416,448,480},{16,48,80,..., dimensions={0} | all-to-all | bytes 1310720 | tf_op jit(solution)/shard_map/all_to_all | solution.py:104
  91.7 11.7 %collective-permute-start.1 = (f32[80,128]{1,0:T(8,128)S(1)}, f32[80,128]{1,0:T(8,128)S(1)}, u32[]{:S(2)}, u32[]{:S(2)}) collective-permute-start(f32[80,128]{1,0:T(8,128)S(1)} %shard_map.62.x_ref), channel_id=1, source_target_pairs={{0,16},{16,0},{32,48},{48,32},{64,80},{80,64},{96,112},{112,96},{1... | collective-permute-start | bytes 122888 | tf_op jit(solution)/shard_map/ppermute | solution.py:106
  103.4 0.8 collective-permute-done.1.y_ref
  104.3 15.2 %all_to_all.37 = f32[16,80,128]{2,1,0:T(8,128)S(1)} all-to-all(f32[16,80,128]{2,1,0:T(8,128)S(1)} %shard_map.63), channel_id=1, replica_groups={{0,32,64,96,128,160,192,224,256,288,320,352,384,416,448,480},{16,48,80,..., dimensions={0} | all-to-all | bytes 1310720 | tf_op jit(solution)/shard_map/all_to_all | solution.py:108
  119.6 0.7 shard_map.65
  120.3 3.2 %collective-permute-start.2 = (f32[576,128]{1,0:T(8,128)S(1)}, f32[576,128]{1,0:T(8,128)S(1)}, u32[]{:S(2)}, u32[]{:S(2)}) collective-permute-start(f32[576,128]{1,0:T(8,128)S(1)} %shard_map.65), channel_id=1, source_target_pairs={{0,1},{1,0},{2,3},{3,2},{4,5},{5,4},{6,7},{7,6},{8,9},{9,8},{10,11... | collective-permute-start | bytes 884744 | tf_op jit(solution)/shard_map/ppermute | solution.py:113
  123.5 0.7 shard_map.64
  124.2 5.0 %collective-permute-done.2 = f32[576,128]{1,0:T(8,128)S(1)} collective-permute-done((f32[576,128]{1,0:T(8,128)S(1)}, f32[576,128]{1,0:T(8,128)S(1)}, u32[]{:S(2)}, u32[]{:S(2)}) %collective-permute-start.2) | collective-permute-done | bytes 294944 | tf_op jit(solution)/shard_map/ppermute | solution.py:113
  129.2 0.7 add.14
  129.9 5.4 %all-to-all-start.3 = ((f32[8,72,128]{2,1,0:T(8,128)}), f32[8,72,128]{2,1,0:T(8,128)S(1)}, u32[]{:S(2)}, u32[]{:S(2)}) async-start(f32[8,72,128]{2,1,0:T(8,128)} %bitcast.5), calls=%async_computation.3 | async-start | bytes 589824 | tf_op jit(solution)/shard_map/all_to_all | solution.py:115
  135.3 9.4 %shard_map.67.x_ref = f32[256,256]{1,0:T(8,128)S(1)} custom-call(f32[1280,128]{1,0:T(8,128)S(1)} %bitcast.14), custom_call_target="tpu_custom_call" | custom-call | flops 20000000000 | bytes 655360 | tf_op jit(solution)/shard_map/pallas_call | solution.py:51
  144.7 10.0 %all-to-all-done.3.x_ref = f32[8,72,128]{2,1,0:T(8,128)S(1)} async-done(((f32[8,72,128]{2,1,0:T(8,128)}), f32[8,72,128]{2,1,0:T(8,128)S(1)}, u32[]{:S(2)}, u32[]{:S(2)}) %all-to-all-start.3) | async-done | bytes 294944 | tf_op jit(solution)/shard_map/all_to_all | solution.py:115
  154.8 24.5 %all-gather.1 = f32[1152,128]{1,0:T(8,128)S(1)} all-gather(f32[72,128]{1,0:T(8,128)S(1)} %shard_map.66), channel_id=3, replica_groups=mesh['fsdp'=32,'tp'=16] {'tp'}, dimensions={0}, use_global_device_ids=true | all-gather | bytes 626688 | tf_op jit(solution)/shard_map/all_gather | solution.py:119
  179.3 1.8 shard_map.68
  181.1 12.4 %all_to_all.38.x_ref = f32[16,80,128]{2,1,0:T(8,128)S(1)} all-to-all(f32[16,80,128]{2,1,0:T(8,128)S(1)} %bitcast.20), channel_id=1, replica_groups={{0,32,64,96,128,160,192,224,256,288,320,352,384,416,448,480},{16,48,80,..., dimensions={0} | all-to-all | bytes 1310720 | tf_op jit(solution)/shard_map/all_to_all | solution.py:104
  193.5 13.2 %collective-permute-start.3 = (f32[80,128]{1,0:T(8,128)S(1)}, f32[80,128]{1,0:T(8,128)S(1)}, u32[]{:S(2)}, u32[]{:S(2)}) collective-permute-start(f32[80,128]{1,0:T(8,128)S(1)} %shard_map.69.x_ref), channel_id=1, source_target_pairs={{0,16},{16,0},{32,48},{48,32},{64,80},{80,64},{96,112},{112,96},{1... | collective-permute-start | bytes 122888 | tf_op jit(solution)/shard_map/ppermute | solution.py:106
  206.8 0.8 collective-permute-done.3.y_ref
  207.7 15.2 %all_to_all.39 = f32[16,80,128]{2,1,0:T(8,128)S(1)} all-to-all(f32[16,80,128]{2,1,0:T(8,128)S(1)} %shard_map.70), channel_id=1, replica_groups={{0,32,64,96,128,160,192,224,256,288,320,352,384,416,448,480},{16,48,80,..., dimensions={0} | all-to-all | bytes 1310720 | tf_op jit(solution)/shard_map/all_to_all | solution.py:108
  222.9 9.4 %shard_map.71.x_ref = f32[256,256]{1,0:T(8,128)S(1)} custom-call(f32[1280,128]{1,0:T(8,128)S(1)} %bitcast.16), custom_call_target="tpu_custom_call" | custom-call | flops 20000000000 | bytes 655360 | tf_op jit(solution)/shard_map/pallas_call | solution.py:51
  232.4 1.3 shard_map.72
  233.7 4.8 %all-to-all-start.6 = ((f32[16,8,128]{2,1,0:T(8,128)}), f32[16,8,128]{2,1,0:T(8,128)S(1)}, u32[]{:S(2)}, u32[]{:S(2)}) async-start(f32[16,8,128]{2,1,0:T(8,128)} %get-tuple-element.24), calls=%async_computation.6 | async-start | bytes 131072 | tf_op jit(solution)/shard_map/all_to_all | solution.py:297
  238.5 1.7 shard_map.74
  240.2 9.9 %all-to-all-done.6.s_ref = f32[16,8,128]{2,1,0:T(8,128)S(1)} async-done(((f32[16,8,128]{2,1,0:T(8,128)}), f32[16,8,128]{2,1,0:T(8,128)S(1)}, u32[]{:S(2)}, u32[]{:S(2)}) %all-to-all-start.6) | async-done | bytes 65568 | tf_op jit(solution)/shard_map/all_to_all | solution.py:297
  250.1 1.7 shard_map.73
  (7 shorter events, 0.2 us)
Async XLA Ops:
  0.6 1.8 copy-start
  3.1 8.5 %collective-permute-start = (f32[576,128]{1,0:T(8,128)S(1)}, f32[576,128]{1,0:T(8,128)S(1)}, u32[]{:S(2)}, u32[]{:S(2)}) collective-permute-start(f32[576,128]{1,0:T(8,128)S(1)} %get-tuple-element.17), channel_id=1, source_target_pairs={{0,1},{1,0},{2,3},{3,2},{4,5},{5,4},{6,7},{7,6},{8,9},{9,8},{10,11... | collective-permute-start | bytes 884744 | tf_op jit(solution)/shard_map/ppermute | solution.py:113
  91.7 12.6 %collective-permute-start.1 = (f32[80,128]{1,0:T(8,128)S(1)}, f32[80,128]{1,0:T(8,128)S(1)}, u32[]{:S(2)}, u32[]{:S(2)}) collective-permute-start(f32[80,128]{1,0:T(8,128)S(1)} %shard_map.62.x_ref), channel_id=1, source_target_pairs={{0,16},{16,0},{32,48},{48,32},{64,80},{80,64},{96,112},{112,96},{1... | collective-permute-start | bytes 122888 | tf_op jit(solution)/shard_map/ppermute | solution.py:106
  120.3 8.9 %collective-permute-start.2 = (f32[576,128]{1,0:T(8,128)S(1)}, f32[576,128]{1,0:T(8,128)S(1)}, u32[]{:S(2)}, u32[]{:S(2)}) collective-permute-start(f32[576,128]{1,0:T(8,128)S(1)} %shard_map.65), channel_id=1, source_target_pairs={{0,1},{1,0},{2,3},{3,2},{4,5},{5,4},{6,7},{7,6},{8,9},{9,8},{10,11... | collective-permute-start | bytes 884744 | tf_op jit(solution)/shard_map/ppermute | solution.py:113
  129.9 24.8 %all-to-all-start.3 = ((f32[8,72,128]{2,1,0:T(8,128)}), f32[8,72,128]{2,1,0:T(8,128)S(1)}, u32[]{:S(2)}, u32[]{:S(2)}) async-start(f32[8,72,128]{2,1,0:T(8,128)} %bitcast.5), calls=%async_computation.3 | async-start | bytes 589824 | tf_op jit(solution)/shard_map/all_to_all | solution.py:115
  193.5 14.1 %collective-permute-start.3 = (f32[80,128]{1,0:T(8,128)S(1)}, f32[80,128]{1,0:T(8,128)S(1)}, u32[]{:S(2)}, u32[]{:S(2)}) collective-permute-start(f32[80,128]{1,0:T(8,128)S(1)} %shard_map.69.x_ref), channel_id=1, source_target_pairs={{0,16},{16,0},{32,48},{48,32},{64,80},{80,64},{96,112},{112,96},{1... | collective-permute-start | bytes 122888 | tf_op jit(solution)/shard_map/ppermute | solution.py:106
  233.7 16.4 %all-to-all-start.6 = ((f32[16,8,128]{2,1,0:T(8,128)}), f32[16,8,128]{2,1,0:T(8,128)S(1)}, u32[]{:S(2)}, u32[]{:S(2)}) async-start(f32[16,8,128]{2,1,0:T(8,128)} %get-tuple-element.24), calls=%async_computation.6 | async-start | bytes 131072 | tf_op jit(solution)/shard_map/all_to_all | solution.py:297
